TPU v7x, 256 devices: a whole 4x4x8 slice. The times are simulated.
256 devices in a mesh: grp: 2 (over core), exp: 16 (over x, y), hid: 8 (over z).
Axes of the slice: x: 4, y: 4, z: 8, core: 2. Of those that a mesh axis runs over, the one named last changes fastest.
Arguments:
- queries: bfloat16 [1024, 48, 128], P(('grp', 'exp', 'hid')), may hold values from -150 to 150
- cache_keys: bfloat16 [1024, 256, 8, 128], P(('grp', 'exp', 'hid')), may hold values from -8 to 8
- cache_values: bfloat16 [1024, 256, 8, 128], P(('grp', 'exp', 'hid')), may hold values from -6 to 6
- new_keys: bfloat16 [1024, 8, 128], P(('grp', 'exp', 'hid')), may hold values from -8 to 8
- new_values: bfloat16 [1024, 8, 128], P(('grp', 'exp', 'hid')), may hold values from -6 to 6
- lengths: int32 [1024], P(('grp', 'exp', 'hid')), may hold values from 1 to 256, 131072 in all
- residual: bfloat16 [1024, 6144], P(('grp', 'exp', 'hid')), may hold values from -6 to 6
- norm_gain: float32 [6144], replicated, may hold values from 0.1 to 1.9
- routes: int32 [1024, 2], P(('grp', 'exp', 'hid')), may hold values from 0 to 7, all different within a row; in each aligned block of 4 rows (0 to 3, 4 to 7, ...) at most 2 rows name the same one
- gate_logits: float32 [1024, 2], P(('grp', 'exp', 'hid')), may hold values from -4 to 4
- w_gate: bfloat16 [8, 6144, 8192], P('hid', None, ('grp', 'exp')), may hold values from -0.078125 to 0.078125
- w_up: bfloat16 [8, 6144, 8192], P('hid', None, ('grp', 'exp')), may hold values from -0.078125 to 0.078125
- w_down: bfloat16 [8, 8192, 6144], P('hid', ('grp', 'exp')), may hold values from -0.0625 to 0.0625
Outputs:
- layer_out: bfloat16 [1024, 6144], P(('grp', 'exp', 'hid'))
Inputs may be any that keep to these rules, and one draw needn't show every extreme that they name: `routes`: each row names two different experts; among the 4 rows of one device no expert is named more than 2 times, and some device names some expert exactly 2 times.
All inputs are finite; a program needn't handle non-finite values. No bound on the sum of `lengths` on one device may be relied on, other than what follows from the above.
Results may differ from a plain program's by a relative error of at most 0.015.
Values may be sent and summed in bfloat16 or wider, within the bound.
A program may use at most 128 MiB of HBM per device.

v0:
```python
import math

import jax
import jax.numpy as jnp
from jax import lax
from jax.sharding import PartitionSpec as P

CAP = 2


def attend(queries, cache_keys, cache_values, new_keys, new_values, lengths):
    count = queries.shape[0]
    kv_heads = cache_keys.shape[2]
    head_size = cache_keys.shape[3]
    slots_cached = cache_keys.shape[1]
    group = queries.shape[1] // kv_heads
    qvals = queries.reshape(count, kv_heads, group, head_size)
    score_scale = 1.0 / math.sqrt(head_size)
    cached = (
        jnp.einsum("rkgd,rtkd->rkgt", qvals, cache_keys, preferred_element_type=jnp.float32)
        * score_scale
    )
    fresh = (
        jnp.einsum("rkgd,rkd->rkg", qvals, new_keys, preferred_element_type=jnp.float32)
        * score_scale
    )
    positions = jnp.arange(slots_cached, dtype=jnp.int32)
    valid = positions[None, :] < lengths[:, None]
    cached = jnp.where(valid[:, None, None, :], cached, jnp.float32(-1e30))
    highest = jnp.maximum(jnp.max(cached, axis=-1), fresh)
    cached_exp = jnp.exp(cached - highest[..., None])
    fresh_exp = jnp.exp(fresh - highest)
    total = jnp.sum(cached_exp, axis=-1) + fresh_exp
    cached_w = (cached_exp / total[..., None]).astype(jnp.bfloat16)
    fresh_w = (fresh_exp / total).astype(jnp.bfloat16)
    result = jnp.einsum(
        "rkgt,rtkd->rkgd", cached_w, cache_values, preferred_element_type=jnp.float32
    )
    result = (
        result
        + fresh_w.astype(jnp.float32)[..., None] * new_values.astype(jnp.float32)[:, :, None, :]
    )
    return result.reshape(count, kv_heads * group * head_size).astype(jnp.bfloat16)


def per_device(
    queries,
    cache_keys,
    cache_values,
    new_keys,
    new_values,
    lengths,
    residual,
    norm_gain,
    routes,
    gate_logits,
    w_gate,
    w_up,
    w_down,
):
    attended = attend(queries, cache_keys, cache_values, new_keys, new_values, lengths)
    mixed = residual.astype(jnp.float32) + attended.astype(jnp.float32)
    normed = (
        mixed * lax.rsqrt(jnp.mean(mixed * mixed, axis=-1, keepdims=True) + 1e-05) * norm_gain
    ).astype(jnp.bfloat16)
    hid_size = lax.axis_size("hid")
    local_experts = w_gate.shape[0]
    experts_all = local_experts * hid_size
    width = normed.shape[1]
    capacity = CAP
    expert_ids = jnp.arange(experts_all, dtype=jnp.int32)
    chosen = routes[:, :, None] == expert_ids[None, None, :]
    gates = jax.nn.softmax(gate_logits, axis=-1)
    combine = jnp.sum(jnp.where(chosen, gates[:, :, None], jnp.float32(0.0)), axis=1)
    selected = jnp.any(chosen, axis=1).astype(jnp.int32)
    ranking = jnp.cumsum(selected, axis=0) - selected
    slot_ids = jnp.arange(capacity, dtype=jnp.int32)
    placement = (selected.T[:, None, :] == 1) & (ranking.T[:, None, :] == slot_ids[None, :, None])
    outgoing = jnp.einsum(
        "ecr,rd->ecd", placement.astype(jnp.bfloat16), normed, preferred_element_type=jnp.float32
    ).astype(jnp.bfloat16)
    outgoing = outgoing.reshape(hid_size, local_experts, capacity, width)
    arrived = lax.all_to_all(outgoing, "hid", split_axis=0, concat_axis=0, tiled=True)
    shard_rows = lax.all_gather(arrived[None], ("grp", "exp"), axis=0, tiled=True)
    gate_in = jnp.einsum("knjrd,jdf->knjrf", shard_rows, w_gate, preferred_element_type=jnp.float32)
    up_in = jnp.einsum("knjrd,jdf->knjrf", shard_rows, w_up, preferred_element_type=jnp.float32)
    hidden_act = (jax.nn.silu(gate_in) * up_in).astype(jnp.bfloat16)
    unit = local_experts * capacity
    own_rows = hid_size * unit
    flat_hidden = hidden_act.reshape(-1, local_experts, capacity, hidden_act.shape[-1])
    product = jnp.einsum("njrf,jfd->njrd", flat_hidden, w_down, preferred_element_type=jnp.float32)
    whole_sum = lax.psum(
        product.reshape(flat_hidden.shape[0] * unit, width).astype(jnp.bfloat16), ("grp", "exp")
    ).astype(jnp.float32)
    summed = lax.dynamic_slice_in_dim(
        whole_sum, lax.axis_index(("grp", "exp")) * own_rows, own_rows, 0
    )
    expert_out = summed.astype(jnp.bfloat16).reshape(hid_size, unit, width)
    returned = lax.all_to_all(expert_out, "hid", split_axis=0, concat_axis=0, tiled=True)
    mixing = placement.astype(jnp.float32) * combine.T[:, None, :]
    moe = jnp.einsum("ecr,ecd->rd", mixing, returned.astype(jnp.float32))
    return (mixed + moe).astype(jnp.bfloat16)


def solution(mesh):
    in_specs = (
        P(("grp", "exp", "hid"), None, None),
        P(("grp", "exp", "hid"), None, None, None),
        P(("grp", "exp", "hid"), None, None, None),
        P(("grp", "exp", "hid"), None, None),
        P(("grp", "exp", "hid"), None, None),
        P(("grp", "exp", "hid")),
        P(("grp", "exp", "hid"), None),
        P(),
        P(("grp", "exp", "hid"), None),
        P(("grp", "exp", "hid"), None),
        P("hid", None, ("grp", "exp")),
        P("hid", None, ("grp", "exp")),
        P("hid", ("grp", "exp"), None),
    )
    out_specs = P(("grp", "exp", "hid"), None)
    return jax.shard_map(
        per_device, mesh=mesh, in_specs=in_specs, out_specs=out_specs, check_vma=False
    )
```

profile of v0, /device:TPU:6, one launch (start us, length us, event | category | flops | bytes accessed | tf_op | source)
XLA Modules:
  0.0 285.8 jit_solution(9803072293108422501)
XLA Ops:
  6.5 0.0 copy-start
  6.5 0.0 all-gather.3.cloned.1.call-start
  6.5 0.0 copy-start.7
  6.5 1.0 copy.54
  7.5 0.9 iota_compare_fusion.2
  8.4 0.8 fusion.56
  9.2 0.0 copy-start.1
  9.3 0.0 copy-start.4
  9.3 0.0 copy-start.2
  9.3 2.3 fusion.80
  11.6 0.2 fusion.52
  11.9 0.7 convert_element_type.71
  12.6 0.0 copy-done.7
  12.6 0.4 fusion.47
  13.0 0.1 reshape.83
  13.1 0.0 copy-done.1
  13.1 0.2 multiply_reduce_fusion
  13.3 0.0 copy-done.4
  13.3 0.1 fusion.67
  13.4 0.0 copy-done.2
  13.4 0.3 fusion.1
  13.7 0.2 copy.58
  13.9 18.7 %all_to_all.10 = bf16[8,1,2,6144]{3,2,1,0:T(2,128)(2,1)S(1)} all-to-all(bf16[8,1,2,6144]{3,2,1,0:T(2,128)(2,1)S(1)} %copy.58), channel_id=1, replica_groups=mesh['grp'=2,'exp'=16,'hid'=8] {'hid'}, dimensions={0} | all-to-all | bytes 393216 | tf_op jit(solution)/shard_map/all_to_all | solution.py:83
  32.6 0.7 copy.59
  33.4 0.0 all-gather.3.cloned.1.call-update
  33.4 0.0 all-reduce.2.cloned.1.call-start
  33.4 49.8 %all-gather.3.cloned.1.call-done = bf16[256,1,2,6144]{3,0,2,1:T(8,128)(2,1)} async-done(((bf16[8,1,2,6144]{3,0,2,1:T(8,128)(2,1)}), bf16[256,1,2,6144]{3,0,2,1:T(8,128)(2,1)}) %all-gather.3.cloned.1.call-update) | async-done | bytes 6291472 | tf_op jit(solution)/shard_map/all_gather | solution.py:84
  83.2 0.0 copy-start.5
  83.2 0.0 copy-start.6
  83.2 5.6 %fusion.15 = f32[32,8,1,2,256]{4,1,3,0,2:T(8,128)S(1)} fusion(bf16[1,6144,256]{2,1,0:T(8,128)(2,1)} %param.23, bf16[256,1,2,6144]{3,0,2,1:T(8,128)(2,1)} %all-gather.3.cloned.1.call-done), kind=kOutput, calls=%fused_computation.18 | convolution fusion | flops 1610612736 | bytes 9961472 | tf_op jit(solution)/shard_map/knjrd,jdf->knjrf/dot_general | solution.py:85
  88.9 0.0 copy-done.5
  88.9 0.8 copy-done.6
  89.6 1.8 fusion.30
  91.4 0.0 copy-done
  91.4 1.8 fusion
  93.3 26.3 %copy.63 = bf16[256,1,2,6144]{3,2,0,1:T(2,128)(2,1)} copy(bf16[256,1,2,6144]{3,0,2,1:T(8,128)(2,1)S(1)} %fusion) | data formatting | bytes 12582912 | tf_op jit(solution)/shard_map/convert_element_type | solution.py:93
  119.5 13.3 %convert_element_type.83 = bf16[512,6144]{1,0:T(8,128)(2,1)} reshape(bf16[256,1,2,6144]{3,2,0,1:T(2,128)(2,1)} %copy.63) | data formatting | bytes 12582912 | tf_op jit(solution)/shard_map/convert_element_type | solution.py:93
  132.8 0.0 copy-start.3
  132.8 0.0 all-reduce.2.cloned.1.call-update
  132.9 0.6 copy-done.3
  133.5 126.0 %all-reduce.2.cloned.1.call-done = bf16[512,6144]{1,0:T(8,128)(2,1)} async-done(((bf16[512,6144]{1,0:T(8,128)(2,1)}), bf16[512,6144]{1,0:T(8,128)(2,1)}) %all-reduce.2.cloned.1.call-update) | async-done | bytes 6291472 | tf_op jit(solution)/shard_map/psum | solution.py:92
  259.5 0.9 convert_convert_fusion
  260.5 0.8 reshape.82
  261.3 7.0 %all-to-all-start.1 = ((bf16[8,2,6144]{2,1,0:T(2,128)(2,1)}), bf16[8,2,6144]{2,1,0:T(2,128)(2,1)S(1)}, u32[]{:S(2)}, u32[]{:S(2)}) async-start(bf16[8,2,6144]{2,1,0:T(2,128)(2,1)} %reshape.82), calls=%async_computation.1 | async-start | bytes 393216 | tf_op jit(solution)/shard_map/all_to_all | solution.py:99
  268.3 0.1 select_reduce_fusion
  268.4 9.7 %all-to-all-done.1 = bf16[8,2,6144]{2,1,0:T(2,128)(2,1)S(1)} async-done(((bf16[8,2,6144]{2,1,0:T(2,128)(2,1)}), bf16[8,2,6144]{2,1,0:T(2,128)(2,1)S(1)}, u32[]{:S(2)}, u32[]{:S(2)}) %all-to-all-start.1) | async-done | bytes 196640 | tf_op jit(solution)/shard_map/all_to_all | solution.py:99
  278.1 0.9 fusion.3
  (9 shorter events, 0.1 us)
Async XLA Ops:
  6.5 84.9 %copy-start = (bf16[1,256,6144]{2,1,0:T(8,128)(2,1)S(1)}, bf16[1,256,6144]{2,1,0:T(8,128)(2,1)}, u32[]{:S(2)}) copy-start(bf16[1,256,6144]{2,1,0:T(8,128)(2,1)} %param.25) | copy-start | bytes 9437188
  6.5 76.7 %all-gather.3.cloned.1.call-start = ((), (), s32[]{:S(2)}) async-start(), calls=%async_computation.3 | async-start | bytes 6488064 | tf_op jit(solution)/shard_map/all_gather | solution.py:84
  6.5 6.0 %copy-start.7 = (bf16[4,256,8,128]{3,2,1,0:T(8,128)(2,1)S(1)}, bf16[4,256,8,128]{3,2,1,0:T(8,128)(2,1)}, u32[]{:S(2)}) copy-start(bf16[4,256,8,128]{3,2,1,0:T(8,128)(2,1)} %param.15) | copy-start | bytes 6291460
  9.2 3.8 %copy-start.1 = (bf16[4,6144]{1,0:T(4,128)(2,1)S(1)}, bf16[4,6144]{1,0:T(4,128)(2,1)}, u32[]{:S(2)}) copy-start(bf16[4,6144]{1,0:T(4,128)(2,1)} %param.19) | copy-start | bytes 147460
  9.3 4.0 %copy-start.4 = (s32[4,2]{0,1:T(2,128)S(1)}, s32[4,2]{0,1:T(2,128)}, u32[]{:S(2)}) copy-start(s32[4,2]{0,1:T(2,128)} %param.21) | copy-start | bytes 100
  9.3 4.1 %copy-start.2 = (f32[6144]{0:T(1024)S(1)}, f32[6144]{0:T(1024)}, u32[]{:S(2)}) copy-start(f32[6144]{0:T(1024)} %param.20) | copy-start | bytes 73732
  33.4 226.1 %all-reduce.2.cloned.1.call-start = ((), (), s32[]{:S(2)}) async-start(), calls=%async_computation.2 | async-start | bytes 12582912 | tf_op jit(solution)/shard_map/psum | solution.py:92
  83.2 5.7 %copy-start.5 = (bf16[256,1,2,6144]{3,0,2,1:T(8,128)(2,1)S(1)}, bf16[256,1,2,6144]{3,0,2,1:T(8,128)(2,1)}, u32[]{:S(2)}) copy-start(bf16[256,1,2,6144]{3,0,2,1:T(8,128)(2,1)} %all-gather.3.cloned.1.call-done) | copy-start | bytes 18874372
  83.2 6.4 %copy-start.6 = (bf16[1,6144,256]{2,1,0:T(8,128)(2,1)S(1)}, bf16[1,6144,256]{2,1,0:T(8,128)(2,1)}, u32[]{:S(2)}) copy-start(bf16[1,6144,256]{2,1,0:T(8,128)(2,1)} %param.24) | copy-start | bytes 9437188
  132.8 0.7 copy-start.3
  261.3 16.8 %all-to-all-start.1 = ((bf16[8,2,6144]{2,1,0:T(2,128)(2,1)}), bf16[8,2,6144]{2,1,0:T(2,128)(2,1)S(1)}, u32[]{:S(2)}, u32[]{:S(2)}) async-start(bf16[8,2,6144]{2,1,0:T(2,128)(2,1)} %reshape.82), calls=%async_computation.1 | async-start | bytes 393216 | tf_op jit(solution)/shard_map/all_to_all | solution.py:99
Sparse Core Ops, SparseCore 0:
  33.5 49.6 all-gather.2
  133.0 126.4 all-reduce.1
where the time goes:
time: 286 us
  waiting for transfers between devices  185 us (65%)
  local copies, waits for them, and re-layouts  43.8 us (15%)
  blocking collectives  18.7 us (7%)
  matrix products  14 us (5%)
  between operations  13.6 us (5%)
  starting transfers between devices  7.06 us (2%)
  other arithmetic  3.21 us (1%)
    psum x1, waiting for transfers between devices, per_device(): lax.psum(product.reshape(flat_hidden.shape[0] * unit, width).astype(jnp.b...  126 us
    all_gather x1, waiting for transfers between devices, per_device(): lax.all_gather(arrived[None], ('grp', 'exp'), axis=0, tiled=True)  49.8 us
    convert_element_type x2, local copies, waits for them, and re-layouts, per_device(): product.reshape(flat_hidden.shape[0] * unit, width).astype(jnp.bfloat16)  39.6 us
    all_to_all x1, blocking collectives, per_device(): lax.all_to_all(outgoing, 'hid', split_axis=0, concat_axis=0, tiled=True)  18.7 us
    all_to_all x1, waiting for transfers between devices, per_device(): lax.all_to_all(expert_out, 'hid', split_axis=0, concat_axis=0, tiled=True)  9.66 us
    all_to_all x1, starting transfers between devices, per_device(): lax.all_to_all(expert_out, 'hid', split_axis=0, concat_axis=0, tiled=True)  7.01 us
  transfers between devices with their start and end apart: 3, of which 3 were waited for; matrix products, arithmetic and copies ran while one was open for 0% of the time, Pallas kernels for 0%

commit v1 on v0

--- a/solution.py
+++ b/solution.py
@@ -1,11 +1,16 @@
+import functools
 import math
 
 import jax
 import jax.numpy as jnp
 from jax import lax
+from jax.experimental import pallas as pl
+from jax.experimental.pallas import tpu as pltpu
 from jax.sharding import PartitionSpec as P
 
 CAP = 2
+SIDE = 4
+MESH = pl.DeviceIdType.MESH
 
 
 def attend(queries, cache_keys, cache_values, new_keys, new_values, lengths):
@@ -41,6 +46,301 @@
         + fresh_w.astype(jnp.float32)[..., None] * new_values.astype(jnp.float32)[:, :, None, :]
     )
     return result.reshape(count, kv_heads * group * head_size).astype(jnp.bfloat16)
+
+
+def moe_kernel(
+    nk, nz, w,
+    out_in, wg_hbm, wu_hbm, wd_hbm, ret_out,
+    wg, wu, wd, zin, xall, acc_g, acc_u, hid, po, pr, s, t1, t2, t3, zout, zret,
+    w_sem, zs_s, zs_r, p1_s, p1_r, p2_s, p2_r, fw_s, fw_r, dd_s, dd_r,
+    ex_s, ex_r, t1_s, t1_r, t2_s, t2_r, t3_s, t3_r, zo_s, zo_r,
+):
+    g = lax.axis_index("grp")
+    xy = lax.axis_index("exp")
+    z = lax.axis_index("hid")
+    x = xy // SIDE
+    y = xy % SIDE
+    wide = 4 * w
+    bf = jnp.bfloat16
+    f32 = jnp.float32
+
+    def at_x(d):
+        return (g, ((x + d) % SIDE) * SIDE + y, z)
+
+    def at_y(d):
+        return (g, x * SIDE + (y + d) % SIDE, z)
+
+    def at_z(d):
+        return (g, xy, (z + d) % nz)
+
+    partner = (1 - g, xy, z)
+    along = (at_x, at_y)
+    across = (at_y, at_x)
+
+    sent = []
+
+    def send(src, dst, ssem, rsem, dev):
+        copy = pltpu.make_async_remote_copy(
+            src_ref=src, dst_ref=dst, send_sem=ssem, recv_sem=rsem,
+            device_id=dev, device_id_type=MESH,
+        )
+        copy.start()
+        sent.append(copy)
+
+    def landed(dst, ssem, rsem, dev):
+        pltpu.make_async_remote_copy(
+            src_ref=dst, dst_ref=dst, send_sem=ssem, recv_sem=rsem,
+            device_id=dev, device_id_type=MESH,
+        ).wait_recv()
+
+    weight_copies = [
+        pltpu.make_async_copy(wg_hbm, wg, w_sem.at[0]),
+        pltpu.make_async_copy(wu_hbm, wu, w_sem.at[1]),
+        pltpu.make_async_copy(wd_hbm, wd, w_sem.at[2]),
+    ]
+    for copy in weight_copies:
+        copy.start()
+
+    barrier = pltpu.get_barrier_semaphore()
+    friends = [partner]
+    friends += [at_x(d) for d in (1, 2, 3)] + [at_y(d) for d in (1, 2, 3)]
+    friends += [at_z(d) for d in range(1, nz)]
+    for dev in friends:
+        pl.semaphore_signal(barrier, inc=1, device_id=dev, device_id_type=MESH)
+    pl.semaphore_wait(barrier, len(friends))
+
+    for k in range(nk):
+        for d in range(1, nz):
+            to = (z + d) % nz
+            send(out_in.at[k, to], zin.at[k, z], zs_s.at[k, d - 1], zs_r.at[k, d - 1], at_z(d))
+        zin[k, z] = out_in[k, z]
+
+    units = nz * 16
+    row = lax.broadcasted_iota(jnp.int32, (units, units), 0)
+    col = lax.broadcasted_iota(jnp.int32, (units, units), 1)
+    spread = (col == (row % 16) * 8 + row // 16).astype(bf)
+    gather = (row == (col % 16) * 8 + col // 16).astype(bf)
+
+    def mine(k, h, d):
+        if h == 0:
+            return xall.at[k, 0, g, :, (y + d) % SIDE]
+        return xall.at[k, 1, g, (x + d) % SIDE]
+
+    def mine_half(k, h, d, side):
+        if h == 0:
+            return xall.at[k, 0, g, pl.ds(2 * side, 2), (y + d) % SIDE]
+        return xall.at[k, 1, g, (x + d) % SIDE, pl.ds(2 * side, 2)]
+
+    def a0(k):
+        for d in range(1, nz):
+            src = (z + nz - d) % nz
+            landed(zin.at[k, src], zs_s.at[k, d - 1], zs_r.at[k, d - 1], at_z(nz - d))
+        block = zin[k].reshape(units, w)
+        block = jnp.dot(spread, block, preferred_element_type=f32).astype(bf)
+        for part in range(8):
+            h, q = part // 4, part % 4
+            xall[k, h, g, x, y, :, q * w:(q + 1) * w] = block[part * 16:(part + 1) * 16]
+        for h in range(2):
+            for d in (1, 3, 2):
+                ref = xall.at[k, h, g, x, y]
+                send(ref, ref, p1_s.at[k, h, d - 1], p1_r.at[k, h, d - 1], along[h](d))
+
+    def a1(k):
+        for h in range(2):
+            for d in (1, 3, 2):
+                if h == 0:
+                    ref = xall.at[k, 0, g, (x + SIDE - d) % SIDE, y]
+                else:
+                    ref = xall.at[k, 1, g, x, (y + SIDE - d) % SIDE]
+                landed(ref, p1_s.at[k, h, d - 1], p1_r.at[k, h, d - 1], along[h](SIDE - d))
+            ref = mine(k, h, 0)
+            send(ref, ref, p2_s.at[k, h, 0], p2_r.at[k, h, 0], across[h](1))
+            send(ref, ref, p2_s.at[k, h, 1], p2_r.at[k, h, 1], across[h](3))
+            send(ref, ref, dd_s.at[k, h, 0], dd_r.at[k, h, 0], partner)
+
+    def a2(k):
+        for h in range(2):
+            for n, d in ((0, 3), (1, 1)):
+                ref = mine(k, h, d)
+                landed(ref, p2_s.at[k, h, n], p2_r.at[k, h, n], across[h](d))
+                half = mine_half(k, h, d, n)
+                send(half, half, fw_s.at[k, h, n], fw_r.at[k, h, n], across[h](SIDE - d))
+                send(ref, ref, dd_s.at[k, h, d], dd_r.at[k, h, d], partner)
+
+    def a3(k):
+        for h in range(2):
+            for n, d in ((0, 3), (1, 1)):
+                half = mine_half(k, h, 2, n)
+                landed(half, fw_s.at[k, h, n], fw_r.at[k, h, n], across[h](d))
+            ref = mine(k, h, 2)
+            send(ref, ref, dd_s.at[k, h, 2], dd_r.at[k, h, 2], partner)
+
+    def m(k):
+        if k == 0:
+            weight_copies[0].wait()
+            weight_copies[1].wait()
+        for h in range(2):
+            for d in range(SIDE):
+                if h == 0:
+                    ref = xall.at[k, 0, 1 - g, :, (y + d) % SIDE]
+                else:
+                    ref = xall.at[k, 1, 1 - g, (x + d) % SIDE]
+                landed(ref, dd_s.at[k, h, d], dd_r.at[k, h, d], partner)
+        first = k * 2 * wide
+
+        @pl.loop(0, 2)
+        def _(i):
+            gate, up = None, None
+            for h in range(2):
+                lhs = xall[k, h, i].reshape(256, wide)
+                rows = slice(first + h * wide, first + (h + 1) * wide)
+                a = jnp.dot(lhs, wg[rows, :], preferred_element_type=f32)
+                b = jnp.dot(lhs, wu[rows, :], preferred_element_type=f32)
+                gate = a if gate is None else gate + a
+                up = b if up is None else up + b
+            if k > 0:
+                gate = gate + acc_g[i]
+                up = up + acc_u[i]
+            if k < nk - 1:
+                acc_g[i] = gate
+                acc_u[i] = up
+            else:
+                hid[i] = (gate * jax.nn.sigmoid(gate) * up).astype(bf)
+
+    def down(k):
+        if k == 0:
+            weight_copies[2].wait()
+        for whose in range(2):
+            lhs = hid[(1 - g) if whose == 0 else g]
+            for h in range(2):
+                cols = slice((2 * k + h) * wide, (2 * k + h + 1) * wide)
+                part = jnp.dot(lhs, wd[:, cols], preferred_element_type=f32).astype(bf)
+                part = part.reshape(SIDE, SIDE, 16, wide)
+                if whose == 0:
+                    po[k, h] = part
+                    send(po.at[k, h], pr.at[k, h], ex_s.at[k, h], ex_r.at[k, h], partner)
+                else:
+                    s[k, h] = part
+
+    def add(*terms):
+        total = terms[0].astype(f32)
+        for term in terms[1:]:
+            total = total + term.astype(f32)
+        return total.astype(bf)
+
+    def s_block(k, h, d):
+        if h == 0:
+            return s.at[k, 0, :, (y + d) % SIDE]
+        return s.at[k, 1, (x + d) % SIDE]
+
+    def s_half(k, h, d, side):
+        if h == 0:
+            return s.at[k, 0, pl.ds(2 * side, 2), (y + d) % SIDE]
+        return s.at[k, 1, (x + d) % SIDE, pl.ds(2 * side, 2)]
+
+    def s1(k):
+        for h in range(2):
+            landed(pr.at[k, h], ex_s.at[k, h], ex_r.at[k, h], partner)
+            s[k, h] = add(s[k, h], pr[k, h])
+            send(s_half(k, h, 2, 0), t1.at[k, h, 0], t1_s.at[k, h, 0], t1_r.at[k, h, 0], across[h](1))
+            send(s_half(k, h, 2, 1), t1.at[k, h, 1], t1_s.at[k, h, 1], t1_r.at[k, h, 1], across[h](3))
+
+    def s2(k):
+        for h in range(2):
+            for n, d in ((0, 1), (1, 3)):
+                landed(t1.at[k, h, n], t1_s.at[k, h, n], t1_r.at[k, h, n], across[h](SIDE - d))
+                half = s_half(k, h, d, n)
+                half[...] = add(half[...], t1[k, h, n])
+                send(s_block(k, h, d), t2.at[k, h, n], t2_s.at[k, h, n], t2_r.at[k, h, n], across[h](d))
+
+    def s3(k):
+        for h in range(2):
+            for n, d in ((0, 1), (1, 3)):
+                landed(t2.at[k, h, n], t2_s.at[k, h, n], t2_r.at[k, h, n], across[h](SIDE - d))
+            block = s_block(k, h, 0)
+            block[...] = add(block[...], t2[k, h, 0], t2[k, h, 1])
+            for d in (1, 3, 2):
+                if h == 0:
+                    src = s.at[k, 0, (x + d) % SIDE, y]
+                else:
+                    src = s.at[k, 1, x, (y + d) % SIDE]
+                send(src, t3.at[k, h, d - 1], t3_s.at[k, h, d - 1], t3_r.at[k, h, d - 1], along[h](d))
+
+    def s4(k):
+        parts = []
+        for h in range(2):
+            for d in (1, 3, 2):
+                landed(t3.at[k, h, d - 1], t3_s.at[k, h, d - 1], t3_r.at[k, h, d - 1], along[h](SIDE - d))
+            total = add(s[k, h, x, y], t3[k, h, 0], t3[k, h, 1], t3[k, h, 2])
+            parts += [total[:, q * w:(q + 1) * w] for q in range(4)]
+        block = jnp.concatenate(parts, axis=0)
+        block = jnp.dot(gather, block, preferred_element_type=f32).astype(bf)
+        zout[k] = block.reshape(nz, 16, w)
+        for d in range(1, nz):
+            to = (z + d) % nz
+            send(zout.at[k, to], zret.at[k, z], zo_s.at[k, d - 1], zo_r.at[k, d - 1], at_z(d))
+        zret[k, z] = zout[k, z]
+
+    def s5(k):
+        for d in range(1, nz):
+            src = (z + nz - d) % nz
+            landed(zret.at[k, src], zo_s.at[k, d - 1], zo_r.at[k, d - 1], at_z(nz - d))
+        ret_out[k] = zret[k]
+
+    def run(stages):
+        for t in range(nk + len(stages) - 1):
+            for j, stage in enumerate(stages):
+                if 0 <= t - j < nk:
+                    stage(t - j)
+
+    run([a0, a1, a2, a3, m])
+    run([down, s1, s2, s3, s4, s5])
+    for copy in sent:
+        copy.wait_send()
+
+
+def experts(outgoing, w_gate, w_up, w_down, nk):
+    nz = outgoing.shape[1]
+    w = outgoing.shape[3]
+    wide = 4 * w
+    width, slice_size = w_gate.shape
+    bf = jnp.bfloat16
+    dma = pltpu.SemaphoreType.DMA
+    vmem = pltpu.VMEM
+    blocks = (nk, 2, SIDE, SIDE, 16, wide)
+    scratch = [
+        vmem((width, slice_size), bf),
+        vmem((width, slice_size), bf),
+        vmem((slice_size, width), bf),
+        vmem((nk, nz, 16, w), bf),
+        vmem((nk, 2, 2, SIDE, SIDE, 16, wide), bf),
+        vmem((2, 256, slice_size), jnp.float32),
+        vmem((2, 256, slice_size), jnp.float32),
+        vmem((2, 256, slice_size), bf),
+        vmem(blocks, bf),
+        vmem(blocks, bf),
+        vmem(blocks, bf),
+        vmem((nk, 2, 2, 2, 16, wide), bf),
+        vmem((nk, 2, 2, 4, 16, wide), bf),
+        vmem((nk, 2, 3, 16, wide), bf),
+        vmem((nk, nz, 16, w), bf),
+        vmem((nk, nz, 16, w), bf),
+        dma((3,)),
+    ]
+    for shape in [(nk, nz - 1), (nk, 2, 3), (nk, 2, 2), (nk, 2, 2), (nk, 2, 4),
+                  (nk, 2), (nk, 2, 2), (nk, 2, 2), (nk, 2, 3), (nk, nz - 1)]:
+        scratch += [dma(shape), dma(shape)]
+    any_spec = pl.BlockSpec(memory_space=pl.ANY)
+    return pl.pallas_call(
+        functools.partial(moe_kernel, nk, nz, w),
+        out_shape=jax.ShapeDtypeStruct(outgoing.shape, bf),
+        in_specs=[pl.BlockSpec(memory_space=pltpu.VMEM), any_spec, any_spec, any_spec],
+        out_specs=pl.BlockSpec(memory_space=pltpu.VMEM),
+        scratch_shapes=scratch,
+        compiler_params=pltpu.CompilerParams(
+            collective_id=0, has_side_effects=True, vmem_limit_bytes=48 * 1024 * 1024
+        ),
+    )(outgoing, w_gate, w_up, w_down)
 
 
 def per_device(
@@ -63,40 +363,24 @@
     normed = (
         mixed * lax.rsqrt(jnp.mean(mixed * mixed, axis=-1, keepdims=True) + 1e-05) * norm_gain
     ).astype(jnp.bfloat16)
-    hid_size = lax.axis_size("hid")
-    local_experts = w_gate.shape[0]
-    experts_all = local_experts * hid_size
+    nz = lax.axis_size("hid")
     width = normed.shape[1]
-    capacity = CAP
-    expert_ids = jnp.arange(experts_all, dtype=jnp.int32)
+    nk = 3
+    w = width // (8 * nk)
+    expert_ids = jnp.arange(nz, dtype=jnp.int32)
     chosen = routes[:, :, None] == expert_ids[None, None, :]
     gates = jax.nn.softmax(gate_logits, axis=-1)
     combine = jnp.sum(jnp.where(chosen, gates[:, :, None], jnp.float32(0.0)), axis=1)
     selected = jnp.any(chosen, axis=1).astype(jnp.int32)
     ranking = jnp.cumsum(selected, axis=0) - selected
-    slot_ids = jnp.arange(capacity, dtype=jnp.int32)
+    slot_ids = jnp.arange(CAP, dtype=jnp.int32)
     placement = (selected.T[:, None, :] == 1) & (ranking.T[:, None, :] == slot_ids[None, :, None])
     outgoing = jnp.einsum(
         "ecr,rd->ecd", placement.astype(jnp.bfloat16), normed, preferred_element_type=jnp.float32
     ).astype(jnp.bfloat16)
-    outgoing = outgoing.reshape(hid_size, local_experts, capacity, width)
-    arrived = lax.all_to_all(outgoing, "hid", split_axis=0, concat_axis=0, tiled=True)
-    shard_rows = lax.all_gather(arrived[None], ("grp", "exp"), axis=0, tiled=True)
-    gate_in = jnp.einsum("knjrd,jdf->knjrf", shard_rows, w_gate, preferred_element_type=jnp.float32)
-    up_in = jnp.einsum("knjrd,jdf->knjrf", shard_rows, w_up, preferred_element_type=jnp.float32)
-    hidden_act = (jax.nn.silu(gate_in) * up_in).astype(jnp.bfloat16)
-    unit = local_experts * capacity
-    own_rows = hid_size * unit
-    flat_hidden = hidden_act.reshape(-1, local_experts, capacity, hidden_act.shape[-1])
-    product = jnp.einsum("njrf,jfd->njrd", flat_hidden, w_down, preferred_element_type=jnp.float32)
-    whole_sum = lax.psum(
-        product.reshape(flat_hidden.shape[0] * unit, width).astype(jnp.bfloat16), ("grp", "exp")
-    ).astype(jnp.float32)
-    summed = lax.dynamic_slice_in_dim(
-        whole_sum, lax.axis_index(("grp", "exp")) * own_rows, own_rows, 0
-    )
-    expert_out = summed.astype(jnp.bfloat16).reshape(hid_size, unit, width)
-    returned = lax.all_to_all(expert_out, "hid", split_axis=0, concat_axis=0, tiled=True)
+    outgoing = outgoing.reshape(nz, CAP, nk, 8, w).transpose(2, 0, 1, 3, 4).reshape(nk, nz, 16, w)
+    returned = experts(outgoing, w_gate[0], w_up[0], w_down[0], nk)
+    returned = returned.reshape(nk, nz, CAP, 8, w).transpose(1, 2, 0, 3, 4).reshape(nz, CAP, width)
     mixing = placement.astype(jnp.float32) * combine.T[:, None, :]
     moe = jnp.einsum("ecr,ecd->rd", mixing, returned.astype(jnp.float32))
     return (mixed + moe).astype(jnp.bfloat16)

time: 286 us -> 81.2 us (0.28)
  waiting for transfers between devices: 185 us -> 0 us
  Pallas kernels: 0 us -> 73.7 us
  local copies, waits for them, and re-layouts: 43.8 us -> 3.05 us
  blocking collectives: 18.7 us -> 0 us
  between operations: 13.6 us -> 0.16 us
  matrix products: 14 us -> 2.45 us
  starting transfers between devices: 7.06 us -> 0 us
    psum x1 -> x0, waiting for transfers between devices: 126 us -> none  [per_device(): lax.psum(product.reshape(flat_hidden.shape[0] * unit, width).astype(jnp.b...]
    pallas_call x0 -> x1, Pallas kernels: none -> 73.7 us  [experts(): pl.pallas_call(functools.partial(moe_kernel, nk, nz, w), out_shape=jax.Sh...]
    all_gather x1 -> x0, waiting for transfers between devices: 49.8 us -> none  [per_device(): lax.all_gather(arrived[None], ('grp', 'exp'), axis=0, tiled=True)]
    convert_element_type x2 -> x0, local copies, waits for them, and re-layouts: 39.6 us -> none  [per_device(): product.reshape(flat_hidden.shape[0] * unit, width).astype(jnp.bfloat16)]
    all_to_all x1 -> x0, blocking collectives: 18.7 us -> none  [per_device(): lax.all_to_all(outgoing, 'hid', split_axis=0, concat_axis=0, tiled=True)]
    all_to_all x1 -> x0, waiting for transfers between devices: 9.66 us -> none  [per_device(): lax.all_to_all(expert_out, 'hid', split_axis=0, concat_axis=0, tiled=True)]
    dot_general x3 -> x0, matrix products: 9.26 us -> none  [the longest x1 5.65 us: per_device(): jnp.einsum('knjrd,jdf->knjrf', shard_rows, w_gate, preferred_element_type...]
    all_to_all x1 -> x0, starting transfers between devices: 7.01 us -> none  [per_device(): lax.all_to_all(expert_out, 'hid', split_axis=0, concat_axis=0, tiled=True)]
  transfers between devices with their start and end apart: 3 -> 0, of which waited for: 3 -> 0; matrix products, arithmetic and copies ran while one was open for 0% -> 0% of each run, Pallas kernels for 0% -> 0%
where the time goes in v1:
time: 81.2 us; the launch traced here: 81.1 us
  Pallas kernels  73.7 us (91%)
  local copies, waits for them, and re-layouts  3.05 us (4%)
  matrix products  2.45 us (3%)
  other arithmetic  1.73 us (2%)
    pallas_call x1, Pallas kernels, experts(): pl.pallas_call(functools.partial(moe_kernel, nk, nz, w), out_shape=jax.Sh...  73.7 us
    unnamed x19, local copies, waits for them, and re-layouts  2.89 us

profile of v1, /device:TPU:6, one launch (start us, length us, event | category | flops | bytes accessed | tf_op | source)
XLA Modules:
  0.0 81.1 jit_solution(14356928233371950722)
XLA Ops:
  0.0 0.0 copy-start
  0.0 0.0 copy-start.8
  0.0 0.0 copy-start.5
  0.0 0.0 copy-start.7
  0.0 1.0 %copy.28 = bf16[4,48,128]{2,0,1:T(4,128)(2,1)S(1)} copy(bf16[4,48,128]{2,1,0:T(8,128)(2,1)} %param.13) | data formatting | bytes 98304 | tf_op args[0]
  1.0 1.1 %iota_compare_fusion.2 = pred[4,256]{1,0:T(4,128)(4,1)S(1)} fusion(s32[4]{0:T(128)} %param.18), kind=kLoop, calls=%fused_computation.39 | loop fusion | flops 1024 | bytes 1040 | tf_op jit(solution)/shard_map/lt | solution.py:33
  2.0 0.0 copy-done
  2.0 0.7 fusion.48
  2.8 0.0 copy-start.2
  2.8 0.0 copy-done.8
  2.8 0.2 fusion.24
  2.9 0.0 copy-start.6
  3.0 0.0 copy-start.3
  3.0 0.2 fusion.21
  3.2 0.0 copy-done.5
  3.2 0.0 copy-done.7
  3.2 0.4 fusion.18
  3.7 0.1 reshape.62
  3.7 0.0 copy-done.2
  3.8 0.2 multiply_reduce_fusion
  3.9 0.0 copy-done.6
  3.9 0.1 fusion.35
  4.1 0.0 copy-done.3
  4.1 0.3 convolution_convert_fusion
  4.4 0.0 copy-start.1
  4.4 1.9 %copy-done.1 = bf16[1,6144,256]{2,1,0:T(8,128)(2,1)S(1)} copy-done((bf16[1,6144,256]{2,1,0:T(8,128)(2,1)S(1)}, bf16[1,6144,256]{2,1,0:T(8,128)(2,1)}, u32[]{:S(2)}) %copy-start.1) | copy-done | bytes 3145752
  6.3 0.0 copy-start.4
  6.3 73.7 %shard_map.127 = bf16[3,8,16,256]{3,2,1,0:T(8,128)(2,1)S(1)} custom-call(bf16[3,8,16,256]{3,2,1,0:T(8,128)(2,1)S(1)} %bitcast.33, bf16[6144,256]{1,0:T(8,128)(2,1)S(1)} %bitcast.32, bf16[6144,256]{1,0:T(8,128)(2,1)} %bitcast.35, bf16[256,6144]{1,0:T(8,128)(2,1)} %bitcast.36), custom_call_target="tpu_custom_call" | custom-call | tf_op jit(solution)/shard_map/pallas_call | solution.py:334
  80.0 0.1 copy.33
  80.0 0.0 copy-done.4
  80.1 0.1 select_reduce_fusion
  80.2 0.9 %fusion.1 = bf16[4,6144]{1,0:T(4,128)(2,1)} fusion(bf16[8,2,6144]{2,0,1:T(8,128)(2,1)S(1)} %bitcast.37, f32[4,6144]{1,0:T(4,128)S(1)} %reshape.62, bf16[4,6144]{1,0:T(4,128)(2,1)S(1)} %copy-done.2, bf16[8,4]{0,1:T(4,128)(2,1)S(1)} %bitcast.43, s32[8,4]{0,1:T(4,128)S(1)} %subtract_bitcast_fusion, pred[8,4]{0,1:T(4,128)(4,1)S(1)} %get-tuple-element.7), kind=kOutput, calls=%fused_computation.3 | convolution fusion | flops 884928 | bytes 393440 | tf_op jit(solution)/shard_map/ecr,ecd->rd/dot_general | solution.py:385
  (11 shorter events, 0.2 us)
Async XLA Ops:
  0.0 2.0 %copy-start = (bf16[4,256,8,128]{3,2,1,0:T(8,128)(2,1)S(1)}, bf16[4,256,8,128]{3,2,1,0:T(8,128)(2,1)}, u32[]{:S(2)}) copy-start(bf16[4,256,8,128]{3,2,1,0:T(8,128)(2,1)} %param.14) | copy-start | bytes 6291460
  0.0 2.8 %copy-start.8 = (bf16[4,8,128]{2,1,0:T(8,128)(2,1)S(1)}, bf16[4,8,128]{2,1,0:T(8,128)(2,1)}, u32[]{:S(2)}) copy-start(bf16[4,8,128]{2,1,0:T(8,128)(2,1)} %param.16) | copy-start | bytes 24580
  0.0 3.2 %copy-start.5 = (bf16[4,8,128]{2,1,0:T(8,128)(2,1)S(1)}, bf16[4,8,128]{2,1,0:T(8,128)(2,1)}, u32[]{:S(2)}) copy-start(bf16[4,8,128]{2,1,0:T(8,128)(2,1)} %param.17) | copy-start | bytes 24580
  0.0 3.2 %copy-start.7 = (bf16[4,256,8,128]{3,2,1,0:T(8,128)(2,1)S(1)}, bf16[4,256,8,128]{3,2,1,0:T(8,128)(2,1)}, u32[]{:S(2)}) copy-start(bf16[4,256,8,128]{3,2,1,0:T(8,128)(2,1)} %param.15) | copy-start | bytes 6291460
  2.8 1.0 %copy-start.2 = (bf16[4,6144]{1,0:T(4,128)(2,1)S(1)}, bf16[4,6144]{1,0:T(4,128)(2,1)}, u32[]{:S(2)}) copy-start(bf16[4,6144]{1,0:T(4,128)(2,1)} %param.19) | copy-start | bytes 147460
  2.9 1.0 %copy-start.6 = (s32[4,2]{0,1:T(2,128)S(1)}, s32[4,2]{0,1:T(2,128)}, u32[]{:S(2)}) copy-start(s32[4,2]{0,1:T(2,128)} %param.21) | copy-start | bytes 100
  3.0 1.1 %copy-start.3 = (f32[6144]{0:T(1024)S(1)}, f32[6144]{0:T(1024)}, u32[]{:S(2)}) copy-start(f32[6144]{0:T(1024)} %param.20) | copy-start | bytes 73732
  4.4 1.9 %copy-start.1 = (bf16[1,6144,256]{2,1,0:T(8,128)(2,1)S(1)}, bf16[1,6144,256]{2,1,0:T(8,128)(2,1)}, u32[]{:S(2)}) copy-start(bf16[1,6144,256]{2,1,0:T(8,128)(2,1)} %param.23) | copy-start | bytes 9437188
  6.3 73.8 %copy-start.4 = (f32[4,2]{0,1:T(2,128)S(1)}, f32[4,2]{0,1:T(2,128)}, u32[]{:S(2)}) copy-start(f32[4,2]{0,1:T(2,128)} %param.22) | copy-start | bytes 100

commit v2 on v1

v2 whole, which is shorter than its diff:
```python
import functools
import math

import jax
import jax.numpy as jnp
from jax import lax
from jax.experimental import pallas as pl
from jax.experimental.pallas import tpu as pltpu
from jax.sharding import PartitionSpec as P

CAP = 2
SIDE = 4
MESH = pl.DeviceIdType.MESH


def attend(queries, cache_keys, cache_values, new_keys, new_values, lengths):
    count = queries.shape[0]
    kv_heads = cache_keys.shape[2]
    head_size = cache_keys.shape[3]
    slots_cached = cache_keys.shape[1]
    group = queries.shape[1] // kv_heads
    qvals = queries.reshape(count, kv_heads, group, head_size)
    score_scale = 1.0 / math.sqrt(head_size)
    cached = (
        jnp.einsum("rkgd,rtkd->rkgt", qvals, cache_keys, preferred_element_type=jnp.float32)
        * score_scale
    )
    fresh = (
        jnp.einsum("rkgd,rkd->rkg", qvals, new_keys, preferred_element_type=jnp.float32)
        * score_scale
    )
    positions = jnp.arange(slots_cached, dtype=jnp.int32)
    valid = positions[None, :] < lengths[:, None]
    cached = jnp.where(valid[:, None, None, :], cached, jnp.float32(-1e30))
    highest = jnp.maximum(jnp.max(cached, axis=-1), fresh)
    cached_exp = jnp.exp(cached - highest[..., None])
    fresh_exp = jnp.exp(fresh - highest)
    total = jnp.sum(cached_exp, axis=-1) + fresh_exp
    cached_w = (cached_exp / total[..., None]).astype(jnp.bfloat16)
    fresh_w = (fresh_exp / total).astype(jnp.bfloat16)
    result = jnp.einsum(
        "rkgt,rtkd->rkgd", cached_w, cache_values, preferred_element_type=jnp.float32
    )
    result = (
        result
        + fresh_w.astype(jnp.float32)[..., None] * new_values.astype(jnp.float32)[:, :, None, :]
    )
    return result.reshape(count, kv_heads * group * head_size).astype(jnp.bfloat16)


def moe_kernel(ws, nz, *refs):
    bf = jnp.bfloat16
    f32 = jnp.float32
    nk = len(ws)
    chunks = range(nk)
    starts = [8 * sum(ws[:k]) for k in chunks]
    refs = list(refs)
    lanes = [pl.ds(start // 8, w) for start, w in zip(starts, ws)]

    def take(n):
        got = refs[:n]
        del refs[:n]
        return got

    out_in, wg_hbm, wu_hbm, wd_hbm, ret_out = take(5)
    wg, wu, wd, acc_g, acc_u, hid = take(6)
    zin, xall, po, pr, part, t1, t2, t3, zout, zret = [take(nk) for _ in range(10)]
    (w_sem, zs_s, zs_r, p1_s, p1_r, p2_s, p2_r, fw_s, fw_r, dd_s, dd_r,
     ex_s, ex_r, t1_s, t1_r, t2_s, t2_r, t3_s, t3_r, zo_s, zo_r) = refs

    g = lax.axis_index("grp")
    xy = lax.axis_index("exp")
    z = lax.axis_index("hid")
    x = xy // SIDE
    y = xy % SIDE

    def at_x(d):
        return (g, ((x + d) % SIDE) * SIDE + y, z)

    def at_y(d):
        return (g, x * SIDE + (y + d) % SIDE, z)

    def at_z(d):
        return (g, xy, (z + d) % nz)

    partner = (1 - g, xy, z)
    along = (at_x, at_y)
    across = (at_y, at_x)
    far_first = (2, 1, 3)
    z_far_first = sorted(range(1, nz), key=lambda d: -min(d, nz - d))

    sent = []

    def send(src, dst, ssem, rsem, dev):
        copy = pltpu.make_async_remote_copy(
            src_ref=src, dst_ref=dst, send_sem=ssem, recv_sem=rsem,
            device_id=dev, device_id_type=MESH,
        )
        copy.start()
        sent.append(copy)

    def landed(dst, ssem, rsem, dev):
        pltpu.make_async_remote_copy(
            src_ref=dst, dst_ref=dst, send_sem=ssem, recv_sem=rsem,
            device_id=dev, device_id_type=MESH,
        ).wait_recv()

    barrier = pltpu.get_barrier_semaphore()
    friends = [partner]
    friends += [at_x(d) for d in (1, 2, 3)] + [at_y(d) for d in (1, 2, 3)]
    friends += [at_z(d) for d in range(1, nz)]
    for dev in friends:
        pl.semaphore_signal(barrier, inc=1, device_id=dev, device_id_type=MESH)
    weight_copies = [
        pltpu.make_async_copy(wg_hbm, wg, w_sem.at[0]),
        pltpu.make_async_copy(wu_hbm, wu, w_sem.at[1]),
        pltpu.make_async_copy(wd_hbm, wd, w_sem.at[2]),
    ]
    for copy in weight_copies:
        copy.start()
    pl.semaphore_wait(barrier, len(friends))

    for k in chunks:
        for d in z_far_first:
            to = (z + d) % nz
            send(out_in.at[to, :, lanes[k]], zin[k].at[z], zs_s.at[k, d - 1], zs_r.at[k, d - 1], at_z(d))
    for k in chunks:
        zin[k][z] = out_in[z, :, lanes[k]]

    units = nz * 16
    row = lax.broadcasted_iota(jnp.int32, (units, units), 0)
    col = lax.broadcasted_iota(jnp.int32, (units, units), 1)
    spread = (col == (row % 16) * 8 + row // 16).astype(bf)
    gather = (row == (col % 16) * 8 + col // 16).astype(bf)

    def mine(k, h, d):
        if h == 0:
            return xall[k].at[0, g, :, (y + d) % SIDE]
        return xall[k].at[1, g, (x + d) % SIDE]

    def mine_half(k, h, d, side):
        if h == 0:
            return xall[k].at[0, g, pl.ds(2 * side, 2), (y + d) % SIDE]
        return xall[k].at[1, g, (x + d) % SIDE, pl.ds(2 * side, 2)]

    def a0(k):
        w = ws[k]
        for d in z_far_first[::-1]:
            src = (z + nz - d) % nz
            landed(zin[k].at[src], zs_s.at[k, d - 1], zs_r.at[k, d - 1], at_z(nz - d))
        block = zin[k][...].reshape(units, w)
        block = jnp.dot(spread, block, preferred_element_type=f32).astype(bf)
        for n in range(8):
            h, q = n // 4, n % 4
            xall[k][h, g, x, y, :, q * w:(q + 1) * w] = block[n * 16:(n + 1) * 16]
        for h in range(2):
            for d in far_first:
                ref = xall[k].at[h, g, x, y]
                send(ref, ref, p1_s.at[k, h, d - 1], p1_r.at[k, h, d - 1], along[h](d))

    def a1(k):
        for h in range(2):
            for d in far_first:
                if h == 0:
                    ref = xall[k].at[0, g, (x + SIDE - d) % SIDE, y]
                else:
                    ref = xall[k].at[1, g, x, (y + SIDE - d) % SIDE]
                landed(ref, p1_s.at[k, h, d - 1], p1_r.at[k, h, d - 1], along[h](SIDE - d))
            ref = mine(k, h, 0)
            send(ref, ref, p2_s.at[k, h, 0], p2_r.at[k, h, 0], across[h](1))
            send(ref, ref, p2_s.at[k, h, 1], p2_r.at[k, h, 1], across[h](3))
            send(ref, ref, dd_s.at[k, h, 0], dd_r.at[k, h, 0], partner)

    def a2(k):
        for h in range(2):
            for n, d in ((0, 3), (1, 1)):
                ref = mine(k, h, d)
                landed(ref, p2_s.at[k, h, n], p2_r.at[k, h, n], across[h](d))
                half = mine_half(k, h, d, n)
                send(half, half, fw_s.at[k, h, n], fw_r.at[k, h, n], across[h](SIDE - d))
                send(ref, ref, dd_s.at[k, h, d], dd_r.at[k, h, d], partner)

    def a3(k):
        for h in range(2):
            for n, d in ((0, 3), (1, 1)):
                half = mine_half(k, h, 2, n)
                landed(half, fw_s.at[k, h, n], fw_r.at[k, h, n], across[h](d))
            ref = mine(k, h, 2)
            send(ref, ref, dd_s.at[k, h, 2], dd_r.at[k, h, 2], partner)

    def m(k):
        wide = 4 * ws[k]
        if k == 0:
            weight_copies[0].wait()
            weight_copies[1].wait()
        for h in range(2):
            for d in range(SIDE):
                if h == 0:
                    ref = xall[k].at[0, 1 - g, :, (y + d) % SIDE]
                else:
                    ref = xall[k].at[1, 1 - g, (x + d) % SIDE]
                landed(ref, dd_s.at[k, h, d], dd_r.at[k, h, d], partner)

        @pl.loop(0, 2)
        def _(i):
            gate, up = None, None
            for h in range(2):
                lhs = xall[k][h, i].reshape(256, wide)
                rows = slice(starts[k] + h * wide, starts[k] + (h + 1) * wide)
                a = jnp.dot(lhs, wg[rows, :], preferred_element_type=f32)
                b = jnp.dot(lhs, wu[rows, :], preferred_element_type=f32)
                gate = a if gate is None else gate + a
                up = b if up is None else up + b
            if k > 0:
                gate = gate + acc_g[i]
                up = up + acc_u[i]
            if k < nk - 1:
                acc_g[i] = gate
                acc_u[i] = up
            else:
                hid[i] = (gate * jax.nn.sigmoid(gate) * up).astype(bf)

    def down(k):
        wide = 4 * ws[k]
        if k == 0:
            weight_copies[2].wait()
        for whose in range(2):
            lhs = hid[(1 - g) if whose == 0 else g]
            for h in range(2):
                cols = slice(starts[k] + h * wide, starts[k] + (h + 1) * wide)
                value = jnp.dot(lhs, wd[:, cols], preferred_element_type=f32).astype(bf)
                value = value.reshape(SIDE, SIDE, 16, wide)
                if whose == 0:
                    po[k][h] = value
                    send(po[k].at[h], pr[k].at[h], ex_s.at[k, h], ex_r.at[k, h], partner)
                else:
                    part[k][h] = value

    def total(*terms):
        value = terms[0][...].astype(f32)
        for term in terms[1:]:
            value = value + term[...].astype(f32)
        return value.astype(bf)

    def block_of(buf, k, h, d):
        if h == 0:
            return buf[k].at[0, :, (y + d) % SIDE]
        return buf[k].at[1, (x + d) % SIDE]

    def half_of(buf, k, h, d, side):
        if h == 0:
            return buf[k].at[0, pl.ds(2 * side, 2), (y + d) % SIDE]
        return buf[k].at[1, (x + d) % SIDE, pl.ds(2 * side, 2)]

    def s1(k):
        for h in range(2):
            landed(pr[k].at[h], ex_s.at[k, h], ex_r.at[k, h], partner)
            block = block_of(part, k, h, 2)
            block[...] = total(block, block_of(pr, k, h, 2))
            for n, d in ((0, 1), (1, 3)):
                send(half_of(part, k, h, 2, n), t1[k].at[h, n], t1_s.at[k, h, n], t1_r.at[k, h, n], across[h](d))

    def s2(k):
        for h in range(2):
            for n, d in ((0, 1), (1, 3)):
                rest = half_of(part, k, h, d, 1 - n)
                rest[...] = total(rest, half_of(pr, k, h, d, 1 - n))
                landed(t1[k].at[h, n], t1_s.at[k, h, n], t1_r.at[k, h, n], across[h](SIDE - d))
                half = half_of(part, k, h, d, n)
                half[...] = total(half, half_of(pr, k, h, d, n), t1[k].at[h, n])
                send(block_of(part, k, h, d), t2[k].at[h, n], t2_s.at[k, h, n], t2_r.at[k, h, n], across[h](d))

    def s3(k):
        for h in range(2):
            for n, d in ((0, 1), (1, 3)):
                landed(t2[k].at[h, n], t2_s.at[k, h, n], t2_r.at[k, h, n], across[h](SIDE - d))
            block = block_of(part, k, h, 0)
            block[...] = total(block, block_of(pr, k, h, 0), t2[k].at[h, 0], t2[k].at[h, 1])
            for d in far_first:
                if h == 0:
                    src = part[k].at[0, (x + d) % SIDE, y]
                else:
                    src = part[k].at[1, x, (y + d) % SIDE]
                send(src, t3[k].at[h, d - 1], t3_s.at[k, h, d - 1], t3_r.at[k, h, d - 1], along[h](d))

    def s4(k):
        w = ws[k]
        parts = []
        for h in range(2):
            for d in far_first[::-1]:
                landed(t3[k].at[h, d - 1], t3_s.at[k, h, d - 1], t3_r.at[k, h, d - 1], along[h](SIDE - d))
            value = total(part[k].at[h, x, y], *[t3[k].at[h, n] for n in range(3)])
            parts += [value[:, q * w:(q + 1) * w] for q in range(4)]
        block = jnp.concatenate(parts, axis=0)
        block = jnp.dot(gather, block, preferred_element_type=f32).astype(bf)
        zout[k][...] = block.reshape(nz, 16, w)
        for d in z_far_first:
            to = (z + d) % nz
            send(zout[k].at[to], zret[k].at[z], zo_s.at[k, d - 1], zo_r.at[k, d - 1], at_z(d))
        zret[k][z] = zout[k][z]

    def s5(k):
        for d in z_far_first[::-1]:
            src = (z + nz - d) % nz
            landed(zret[k].at[src], zo_s.at[k, d - 1], zo_r.at[k, d - 1], at_z(nz - d))
        ret_out[:, :, lanes[k]] = zret[k][...]

    for stage in (a0, a1, a2):
        for k in chunks:
            stage(k)
    for k in range(nk + 1):
        if k < nk:
            a3(k)
        if k > 0:
            m(k - 1)
    for k in range(nk + 1):
        if k < nk:
            down(k)
        if k > 0:
            s1(k - 1)
    for stage in (s2, s3, s4, s5):
        for k in chunks:
            stage(k)
    for copy in sent:
        copy.wait_send()


def experts(outgoing, w_gate, w_up, w_down, ws):
    nz = outgoing.shape[0]
    nk = len(ws)
    width, slice_size = w_gate.shape
    bf = jnp.bfloat16
    dma = pltpu.SemaphoreType.DMA
    vmem = pltpu.VMEM
    scratch = [
        vmem((width, slice_size), bf),
        vmem((width, slice_size), bf),
        vmem((slice_size, width), bf),
        vmem((2, 256, slice_size), jnp.float32),
        vmem((2, 256, slice_size), jnp.float32),
        vmem((2, 256, slice_size), bf),
    ]
    blocks = (2, SIDE, SIDE, 16)
    for lead in ((nz, 16), (2,) + blocks, blocks, blocks, blocks, (2, 2, 2, 16), (2, 2, 4, 16),
                 (2, 3, 16), (nz, 16), (nz, 16)):
        scratch += [vmem(lead + ((w if lead[0] == nz else 4 * w),), bf) for w in ws]
    scratch.append(dma((3,)))
    for shape in [(nk, nz - 1), (nk, 2, 3), (nk, 2, 2), (nk, 2, 2), (nk, 2, 4),
                  (nk, 2), (nk, 2, 2), (nk, 2, 2), (nk, 2, 3), (nk, nz - 1)]:
        scratch += [dma(shape), dma(shape)]
    any_spec = pl.BlockSpec(memory_space=pl.ANY)
    vmem_spec = pl.BlockSpec(memory_space=pltpu.VMEM)
    return pl.pallas_call(
        functools.partial(moe_kernel, ws, nz),
        out_shape=jax.ShapeDtypeStruct(outgoing.shape, bf),
        in_specs=[vmem_spec] + [any_spec] * 3,
        out_specs=vmem_spec,
        scratch_shapes=scratch,
        compiler_params=pltpu.CompilerParams(
            collective_id=0, has_side_effects=True, vmem_limit_bytes=48 * 1024 * 1024
        ),
    )(outgoing, w_gate, w_up, w_down)


def per_device(
    queries,
    cache_keys,
    cache_values,
    new_keys,
    new_values,
    lengths,
    residual,
    norm_gain,
    routes,
    gate_logits,
    w_gate,
    w_up,
    w_down,
):
    attended = attend(queries, cache_keys, cache_values, new_keys, new_values, lengths)
    mixed = residual.astype(jnp.float32) + attended.astype(jnp.float32)
    normed = (
        mixed * lax.rsqrt(jnp.mean(mixed * mixed, axis=-1, keepdims=True) + 1e-05) * norm_gain
    ).astype(jnp.bfloat16)
    nz = lax.axis_size("hid")
    width = normed.shape[1]
    ws = (256, 256, 256)
    expert_ids = jnp.arange(nz, dtype=jnp.int32)
    chosen = routes[:, :, None] == expert_ids[None, None, :]
    gates = jax.nn.softmax(gate_logits, axis=-1)
    combine = jnp.sum(jnp.where(chosen, gates[:, :, None], jnp.float32(0.0)), axis=1)
    selected = jnp.any(chosen, axis=1).astype(jnp.int32)
    ranking = jnp.cumsum(selected, axis=0) - selected
    slot_ids = jnp.arange(CAP, dtype=jnp.int32)
    placement = (selected.T[:, None, :] == 1) & (ranking.T[:, None, :] == slot_ids[None, :, None])
    outgoing = jnp.einsum(
        "ecr,rd->ecd", placement.astype(jnp.bfloat16), normed, preferred_element_type=jnp.float32
    ).astype(jnp.bfloat16)
    ends = [8 * sum(ws[: k + 1]) for k in range(len(ws))]
    outgoing = jnp.concatenate(
        [outgoing[:, :, end - 8 * w:end].reshape(nz, CAP * 8, w) for end, w in zip(ends, ws)],
        axis=-1,
    )
    returned = experts(outgoing, w_gate[0], w_up[0], w_down[0], ws)
    returned = jnp.concatenate(
        [
            returned[:, :, end // 8 - w:end // 8].reshape(nz, CAP, 8 * w)
            for end, w in zip(ends, ws)
        ],
        axis=-1,
    )
    mixing = placement.astype(jnp.float32) * combine.T[:, None, :]
    moe = jnp.einsum("ecr,ecd->rd", mixing, returned.astype(jnp.float32))
    return (mixed + moe).astype(jnp.bfloat16)


def solution(mesh):
    in_specs = (
        P(("grp", "exp", "hid"), None, None),
        P(("grp", "exp", "hid"), None, None, None),
        P(("grp", "exp", "hid"), None, None, None),
        P(("grp", "exp", "hid"), None, None),
        P(("grp", "exp", "hid"), None, None),
        P(("grp", "exp", "hid")),
        P(("grp", "exp", "hid"), None),
        P(),
        P(("grp", "exp", "hid"), None),
        P(("grp", "exp", "hid"), None),
        P("hid", None, ("grp", "exp")),
        P("hid", None, ("grp", "exp")),
        P("hid", ("grp", "exp"), None),
    )
    out_specs = P(("grp", "exp", "hid"), None)
    return jax.shard_map(
        per_device, mesh=mesh, in_specs=in_specs, out_specs=out_specs, check_vma=False
    )
```

time: 81.2 us -> 75.6 us (0.931)
  Pallas kernels: 73.7 us -> 67.2 us
    pallas_call x1, Pallas kernels: 73.7 us -> 67.2 us  [experts(): pl.pallas_call(functools.partial(moe_kernel, ws, nz), out_shape=jax.Shape...]
where the time goes in v2:
time: 75.6 us; the launch traced here: 75.1 us
  Pallas kernels  67.2 us (89%)
  local copies, waits for them, and re-layouts  3.47 us (5%)
  matrix products  2.45 us (3%)
  other arithmetic  1.75 us (2%)
    pallas_call x1, Pallas kernels, experts(): pl.pallas_call(functools.partial(moe_kernel, ws, nz), out_shape=jax.Shape...  67.2 us
    unnamed x19, local copies, waits for them, and re-layouts  2.89 us

profile of v2, /device:TPU:6, one launch (start us, length us, event | category | flops | bytes accessed | tf_op | source)
XLA Modules:
  0.0 75.1 jit_solution(3261766822658730512)
XLA Ops:
  0.0 0.0 copy-start
  0.0 0.0 copy-start.8
  0.0 0.0 copy-start.5
  0.0 0.0 copy-start.7
  0.0 1.0 %copy.36 = bf16[4,48,128]{2,0,1:T(4,128)(2,1)S(1)} copy(bf16[4,48,128]{2,1,0:T(8,128)(2,1)} %param.13) | data formatting | bytes 98304 | tf_op args[0]
  1.0 1.1 %iota_compare_fusion.2 = pred[4,256]{1,0:T(4,128)(4,1)S(1)} fusion(s32[4]{0:T(128)} %param.18), kind=kLoop, calls=%fused_computation.44 | loop fusion | flops 1024 | bytes 1040 | tf_op jit(solution)/shard_map/lt | solution.py:33
  2.0 0.0 copy-done
  2.0 0.7 fusion.56
  2.8 0.0 copy-start.2
  2.8 0.0 copy-done.8
  2.8 0.2 fusion.29
  2.9 0.0 copy-start.6
  3.0 0.0 copy-start.3
  3.0 0.2 fusion.21
  3.2 0.0 copy-done.5
  3.2 0.0 copy-done.7
  3.2 0.4 fusion.18
  3.7 0.1 reshape.70
  3.7 0.0 copy-done.2
  3.8 0.2 multiply_reduce_fusion
  3.9 0.0 copy-done.6
  3.9 0.1 fusion.40
  4.1 0.0 copy-done.3
  4.1 0.3 convolution_convert_fusion
  4.4 0.1 copy.40
  4.5 0.1 copy.41
  4.6 0.1 copy.42
  4.8 0.0 copy-start.1
  4.8 1.9 %copy-done.1 = bf16[1,6144,256]{2,1,0:T(8,128)(2,1)S(1)} copy-done((bf16[1,6144,256]{2,1,0:T(8,128)(2,1)S(1)}, bf16[1,6144,256]{2,1,0:T(8,128)(2,1)}, u32[]{:S(2)}) %copy-start.1) | copy-done | bytes 3145752
  6.7 0.0 copy-start.4
  6.7 67.2 %shard_map.127 = bf16[8,16,768]{2,1,0:T(8,128)(2,1)S(1)} custom-call(bf16[8,16,768]{2,1,0:T(8,128)(2,1)S(1)} %pad_maximum_fusion.refs_0_, bf16[6144,256]{1,0:T(8,128)(2,1)S(1)} %bitcast.21, bf16[6144,256]{1,0:T(8,128)(2,1)} %bitcast.22, bf16[256,6144]{1,0:T(8,128)(2,1)} %bitcast.23), custom_call_target="tpu_custom_call" | custom-call | tf_op jit(solution)/shard_map/pallas_call | solution.py:353
  74.1 0.0 copy-done.4
  74.2 0.1 select_reduce_fusion
  74.3 0.9 %fusion.1 = bf16[4,6144]{1,0:T(4,128)(2,1)} fusion(bf16[8,2,2048]{2,0,1:T(8,128)(2,1)S(1)} %copy.45, bf16[8,2,2048]{2,0,1:T(8,128)(2,1)S(1)} %copy.44, bf16[8,2,2048]{2,0,1:T(8,128)(2,1)S(1)} %copy.43, f32[4,6144]{1,0:T(4,128)S(1)} %reshape.70, bf16[4,6144]{1,0:T(4,128)(2,1)S(1)} %copy-done.2, bf16[8,4]{0,1:T(4,128)(2,1)S(1)} %bitcast.28, ...), kind=kOutput, calls=%fused_computation.3 | convolution fusion | flops 1474752 | bytes 393440 | tf_op jit(solution)/shard_map/ecr,ecd->rd/dot_general | solution.py:413
  (22 shorter events, 0.5 us)
Async XLA Ops:
  0.0 2.0 %copy-start = (bf16[4,256,8,128]{3,2,1,0:T(8,128)(2,1)S(1)}, bf16[4,256,8,128]{3,2,1,0:T(8,128)(2,1)}, u32[]{:S(2)}) copy-start(bf16[4,256,8,128]{3,2,1,0:T(8,128)(2,1)} %param.14) | copy-start | bytes 6291460
  0.0 2.8 %copy-start.8 = (bf16[4,8,128]{2,1,0:T(8,128)(2,1)S(1)}, bf16[4,8,128]{2,1,0:T(8,128)(2,1)}, u32[]{:S(2)}) copy-start(bf16[4,8,128]{2,1,0:T(8,128)(2,1)} %param.16) | copy-start | bytes 24580
  0.0 3.2 %copy-start.5 = (bf16[4,8,128]{2,1,0:T(8,128)(2,1)S(1)}, bf16[4,8,128]{2,1,0:T(8,128)(2,1)}, u32[]{:S(2)}) copy-start(bf16[4,8,128]{2,1,0:T(8,128)(2,1)} %param.17) | copy-start | bytes 24580
  0.0 3.2 %copy-start.7 = (bf16[4,256,8,128]{3,2,1,0:T(8,128)(2,1)S(1)}, bf16[4,256,8,128]{3,2,1,0:T(8,128)(2,1)}, u32[]{:S(2)}) copy-start(bf16[4,256,8,128]{3,2,1,0:T(8,128)(2,1)} %param.15) | copy-start | bytes 6291460
  2.8 1.0 %copy-start.2 = (bf16[4,6144]{1,0:T(4,128)(2,1)S(1)}, bf16[4,6144]{1,0:T(4,128)(2,1)}, u32[]{:S(2)}) copy-start(bf16[4,6144]{1,0:T(4,128)(2,1)} %param.19) | copy-start | bytes 147460
  2.9 1.0 %copy-start.6 = (s32[4,2]{0,1:T(2,128)S(1)}, s32[4,2]{0,1:T(2,128)}, u32[]{:S(2)}) copy-start(s32[4,2]{0,1:T(2,128)} %param.21) | copy-start | bytes 100
  3.0 1.1 %copy-start.3 = (f32[6144]{0:T(1024)S(1)}, f32[6144]{0:T(1024)}, u32[]{:S(2)}) copy-start(f32[6144]{0:T(1024)} %param.20) | copy-start | bytes 73732
  4.8 1.9 %copy-start.1 = (bf16[1,6144,256]{2,1,0:T(8,128)(2,1)S(1)}, bf16[1,6144,256]{2,1,0:T(8,128)(2,1)}, u32[]{:S(2)}) copy-start(bf16[1,6144,256]{2,1,0:T(8,128)(2,1)} %param.23) | copy-start | bytes 9437188
  6.7 67.4 %copy-start.4 = (f32[4,2]{0,1:T(2,128)S(1)}, f32[4,2]{0,1:T(2,128)}, u32[]{:S(2)}) copy-start(f32[4,2]{0,1:T(2,128)} %param.22) | copy-start | bytes 100

commit v3 on v2

--- a/solution.py
+++ b/solution.py
@@ -64,9 +64,9 @@
 
     out_in, wg_hbm, wu_hbm, wd_hbm, ret_out = take(5)
     wg, wu, wd, acc_g, acc_u, hid = take(6)
-    zin, xall, po, pr, part, t1, t2, t3, zout, zret = [take(nk) for _ in range(10)]
-    (w_sem, zs_s, zs_r, p1_s, p1_r, p2_s, p2_r, fw_s, fw_r, dd_s, dd_r,
-     ex_s, ex_r, t1_s, t1_r, t2_s, t2_r, t3_s, t3_r, zo_s, zo_r) = refs
+    zin, xall, part, t1, t2, t3, zout, zret = [take(nk) for _ in range(8)]
+    (w_sem, zs_s, zs_r, p1_s, p1_r, p2_s, p2_r, fw_s, fw_r,
+     ws_s, ws_r, t1_s, t1_r, tf_s, tf_r, t2_s, t2_r, t3_s, t3_r, zo_s, zo_r) = refs
 
     g = lax.axis_index("grp")
     xy = lax.axis_index("exp")
@@ -111,12 +111,11 @@
     friends += [at_z(d) for d in range(1, nz)]
     for dev in friends:
         pl.semaphore_signal(barrier, inc=1, device_id=dev, device_id_type=MESH)
-    weight_copies = [
-        pltpu.make_async_copy(wg_hbm, wg, w_sem.at[0]),
-        pltpu.make_async_copy(wu_hbm, wu, w_sem.at[1]),
-        pltpu.make_async_copy(wd_hbm, wd, w_sem.at[2]),
+    weights = ((wg_hbm, wg), (wu_hbm, wu), (wd_hbm, wd))
+    own_weights = [
+        pltpu.make_async_copy(src, dst.at[g], w_sem.at[n]) for n, (src, dst) in enumerate(weights)
     ]
-    for copy in weight_copies:
+    for copy in own_weights:
         copy.start()
     pl.semaphore_wait(barrier, len(friends))
 
@@ -126,6 +125,13 @@
             send(out_in.at[to, :, lanes[k]], zin[k].at[z], zs_s.at[k, d - 1], zs_r.at[k, d - 1], at_z(d))
     for k in chunks:
         zin[k][z] = out_in[z, :, lanes[k]]
+    for n, (src, dst) in enumerate(weights):
+        send(src, dst.at[g], ws_s.at[n], ws_r.at[n], partner)
+
+    def ready(n):
+        dst = weights[n][1]
+        own_weights[n].wait()
+        landed(dst.at[1 - g], ws_s.at[n], ws_r.at[n], partner)
 
     units = nz * 16
     row = lax.broadcasted_iota(jnp.int32, (units, units), 0)
@@ -133,15 +139,20 @@
     spread = (col == (row % 16) * 8 + row // 16).astype(bf)
     gather = (row == (col % 16) * 8 + col // 16).astype(bf)
 
-    def mine(k, h, d):
-        if h == 0:
-            return xall[k].at[0, g, :, (y + d) % SIDE]
-        return xall[k].at[1, g, (x + d) % SIDE]
-
     def mine_half(k, h, d, side):
         if h == 0:
-            return xall[k].at[0, g, pl.ds(2 * side, 2), (y + d) % SIDE]
-        return xall[k].at[1, g, (x + d) % SIDE, pl.ds(2 * side, 2)]
+            return xall[k].at[0, pl.ds(2 * side, 2), (y + d) % SIDE]
+        return xall[k].at[1, (x + d) % SIDE, pl.ds(2 * side, 2)]
+
+    def came(k, h, j, d):
+        if h == 0:
+            return xall[k].at[0, (x + SIDE - j) % SIDE, (y + d) % SIDE]
+        return xall[k].at[1, (x + d) % SIDE, (y + SIDE - j) % SIDE]
+
+    def pass_on(k, h, j):
+        ref = came(k, h, j, 0)
+        for n, d in ((0, 1), (1, 3)):
+            send(ref, ref, p2_s.at[k, h, n, j], p2_r.at[k, h, n, j], across[h](d))
 
     def a0(k):
         w = ws[k]
@@ -152,63 +163,50 @@
         block = jnp.dot(spread, block, preferred_element_type=f32).astype(bf)
         for n in range(8):
             h, q = n // 4, n % 4
-            xall[k][h, g, x, y, :, q * w:(q + 1) * w] = block[n * 16:(n + 1) * 16]
+            xall[k][h, x, y, :, q * w:(q + 1) * w] = block[n * 16:(n + 1) * 16]
         for h in range(2):
             for d in far_first:
-                ref = xall[k].at[h, g, x, y]
+                ref = xall[k].at[h, x, y]
                 send(ref, ref, p1_s.at[k, h, d - 1], p1_r.at[k, h, d - 1], along[h](d))
+        for h in range(2):
+            pass_on(k, h, 0)
 
     def a1(k):
         for h in range(2):
-            for d in far_first:
-                if h == 0:
-                    ref = xall[k].at[0, g, (x + SIDE - d) % SIDE, y]
-                else:
-                    ref = xall[k].at[1, g, x, (y + SIDE - d) % SIDE]
+            for d in (1, 3, 2):
+                ref = came(k, h, d, 0)
                 landed(ref, p1_s.at[k, h, d - 1], p1_r.at[k, h, d - 1], along[h](SIDE - d))
-            ref = mine(k, h, 0)
-            send(ref, ref, p2_s.at[k, h, 0], p2_r.at[k, h, 0], across[h](1))
-            send(ref, ref, p2_s.at[k, h, 1], p2_r.at[k, h, 1], across[h](3))
-            send(ref, ref, dd_s.at[k, h, 0], dd_r.at[k, h, 0], partner)
+                pass_on(k, h, d)
 
     def a2(k):
         for h in range(2):
             for n, d in ((0, 3), (1, 1)):
-                ref = mine(k, h, d)
-                landed(ref, p2_s.at[k, h, n], p2_r.at[k, h, n], across[h](d))
+                for j in (0, 1, 3, 2):
+                    ref = came(k, h, j, d)
+                    landed(ref, p2_s.at[k, h, n, j], p2_r.at[k, h, n, j], across[h](d))
                 half = mine_half(k, h, d, n)
                 send(half, half, fw_s.at[k, h, n], fw_r.at[k, h, n], across[h](SIDE - d))
-                send(ref, ref, dd_s.at[k, h, d], dd_r.at[k, h, d], partner)
 
     def a3(k):
         for h in range(2):
             for n, d in ((0, 3), (1, 1)):
                 half = mine_half(k, h, 2, n)
                 landed(half, fw_s.at[k, h, n], fw_r.at[k, h, n], across[h](d))
-            ref = mine(k, h, 2)
-            send(ref, ref, dd_s.at[k, h, 2], dd_r.at[k, h, 2], partner)
 
     def m(k):
         wide = 4 * ws[k]
         if k == 0:
-            weight_copies[0].wait()
-            weight_copies[1].wait()
-        for h in range(2):
-            for d in range(SIDE):
-                if h == 0:
-                    ref = xall[k].at[0, 1 - g, :, (y + d) % SIDE]
-                else:
-                    ref = xall[k].at[1, 1 - g, (x + d) % SIDE]
-                landed(ref, dd_s.at[k, h, d], dd_r.at[k, h, d], partner)
+            ready(0)
+            ready(1)
 
         @pl.loop(0, 2)
         def _(i):
             gate, up = None, None
             for h in range(2):
-                lhs = xall[k][h, i].reshape(256, wide)
+                lhs = xall[k][h].reshape(256, wide)
                 rows = slice(starts[k] + h * wide, starts[k] + (h + 1) * wide)
-                a = jnp.dot(lhs, wg[rows, :], preferred_element_type=f32)
-                b = jnp.dot(lhs, wu[rows, :], preferred_element_type=f32)
+                a = jnp.dot(lhs, wg[i, rows, :], preferred_element_type=f32)
+                b = jnp.dot(lhs, wu[i, rows, :], preferred_element_type=f32)
                 gate = a if gate is None else gate + a
                 up = b if up is None else up + b
             if k > 0:
@@ -220,21 +218,12 @@
             else:
                 hid[i] = (gate * jax.nn.sigmoid(gate) * up).astype(bf)
 
-    def down(k):
+    def down(k, h):
         wide = 4 * ws[k]
-        if k == 0:
-            weight_copies[2].wait()
-        for whose in range(2):
-            lhs = hid[(1 - g) if whose == 0 else g]
-            for h in range(2):
-                cols = slice(starts[k] + h * wide, starts[k] + (h + 1) * wide)
-                value = jnp.dot(lhs, wd[:, cols], preferred_element_type=f32).astype(bf)
-                value = value.reshape(SIDE, SIDE, 16, wide)
-                if whose == 0:
-                    po[k][h] = value
-                    send(po[k].at[h], pr[k].at[h], ex_s.at[k, h], ex_r.at[k, h], partner)
-                else:
-                    part[k][h] = value
+        cols = slice(starts[k] + h * wide, starts[k] + (h + 1) * wide)
+        value = jnp.dot(hid[0], wd[0, :, cols], preferred_element_type=f32)
+        value = value + jnp.dot(hid[1], wd[1, :, cols], preferred_element_type=f32)
+        part[k][h] = value.astype(bf).reshape(SIDE, SIDE, 16, wide)
 
     def total(*terms):
         value = terms[0][...].astype(f32)
@@ -253,29 +242,32 @@
         return buf[k].at[1, (x + d) % SIDE, pl.ds(2 * side, 2)]
 
     def s1(k):
-        for h in range(2):
-            landed(pr[k].at[h], ex_s.at[k, h], ex_r.at[k, h], partner)
-            block = block_of(part, k, h, 2)
-            block[...] = total(block, block_of(pr, k, h, 2))
+        if k == 0:
+            ready(2)
+        for h in range(2):
+            down(k, h)
             for n, d in ((0, 1), (1, 3)):
                 send(half_of(part, k, h, 2, n), t1[k].at[h, n], t1_s.at[k, h, n], t1_r.at[k, h, n], across[h](d))
+            for n, d in ((0, 1), (1, 3)):
+                send(half_of(part, k, h, d, 1 - n), t2[k].at[h, n, pl.ds(2 * (1 - n), 2)], tf_s.at[k, h, n], tf_r.at[k, h, n], across[h](d))
 
     def s2(k):
         for h in range(2):
             for n, d in ((0, 1), (1, 3)):
-                rest = half_of(part, k, h, d, 1 - n)
-                rest[...] = total(rest, half_of(pr, k, h, d, 1 - n))
                 landed(t1[k].at[h, n], t1_s.at[k, h, n], t1_r.at[k, h, n], across[h](SIDE - d))
                 half = half_of(part, k, h, d, n)
-                half[...] = total(half, half_of(pr, k, h, d, n), t1[k].at[h, n])
-                send(block_of(part, k, h, d), t2[k].at[h, n], t2_s.at[k, h, n], t2_r.at[k, h, n], across[h](d))
+                half[...] = total(half, t1[k].at[h, n])
+                send(half, t2[k].at[h, n, pl.ds(2 * n, 2)], t2_s.at[k, h, n], t2_r.at[k, h, n], across[h](d))
 
     def s3(k):
         for h in range(2):
             for n, d in ((0, 1), (1, 3)):
-                landed(t2[k].at[h, n], t2_s.at[k, h, n], t2_r.at[k, h, n], across[h](SIDE - d))
+                free = t2[k].at[h, n, pl.ds(2 * (1 - n), 2)]
+                landed(free, tf_s.at[k, h, n], tf_r.at[k, h, n], across[h](SIDE - d))
+                half = t2[k].at[h, n, pl.ds(2 * n, 2)]
+                landed(half, t2_s.at[k, h, n], t2_r.at[k, h, n], across[h](SIDE - d))
             block = block_of(part, k, h, 0)
-            block[...] = total(block, block_of(pr, k, h, 0), t2[k].at[h, 0], t2[k].at[h, 1])
+            block[...] = total(block, t2[k].at[h, 0], t2[k].at[h, 1])
             for d in far_first:
                 if h == 0:
                     src = part[k].at[0, (x + d) % SIDE, y]
@@ -308,17 +300,10 @@
     for stage in (a0, a1, a2):
         for k in chunks:
             stage(k)
-    for k in range(nk + 1):
-        if k < nk:
-            a3(k)
-        if k > 0:
-            m(k - 1)
-    for k in range(nk + 1):
-        if k < nk:
-            down(k)
-        if k > 0:
-            s1(k - 1)
-    for stage in (s2, s3, s4, s5):
+    for k in chunks:
+        a3(k)
+        m(k)
+    for stage in (s1, s2, s3, s4, s5):
         for k in chunks:
             stage(k)
     for copy in sent:
@@ -333,20 +318,20 @@
     dma = pltpu.SemaphoreType.DMA
     vmem = pltpu.VMEM
     scratch = [
-        vmem((width, slice_size), bf),
-        vmem((width, slice_size), bf),
-        vmem((slice_size, width), bf),
+        vmem((2, width, slice_size), bf),
+        vmem((2, width, slice_size), bf),
+        vmem((2, slice_size, width), bf),
         vmem((2, 256, slice_size), jnp.float32),
         vmem((2, 256, slice_size), jnp.float32),
         vmem((2, 256, slice_size), bf),
     ]
     blocks = (2, SIDE, SIDE, 16)
-    for lead in ((nz, 16), (2,) + blocks, blocks, blocks, blocks, (2, 2, 2, 16), (2, 2, 4, 16),
+    for lead in ((nz, 16), blocks, blocks, (2, 2, 2, 16), (2, 2, 4, 16),
                  (2, 3, 16), (nz, 16), (nz, 16)):
         scratch += [vmem(lead + ((w if lead[0] == nz else 4 * w),), bf) for w in ws]
     scratch.append(dma((3,)))
-    for shape in [(nk, nz - 1), (nk, 2, 3), (nk, 2, 2), (nk, 2, 2), (nk, 2, 4),
-                  (nk, 2), (nk, 2, 2), (nk, 2, 2), (nk, 2, 3), (nk, nz - 1)]:
+    for shape in [(nk, nz - 1), (nk, 2, 3), (nk, 2, 2, 4), (nk, 2, 2),
+                  (3,), (nk, 2, 2), (nk, 2, 2), (nk, 2, 2), (nk, 2, 3), (nk, nz - 1)]:
         scratch += [dma(shape), dma(shape)]
     any_spec = pl.BlockSpec(memory_space=pl.ANY)
     vmem_spec = pl.BlockSpec(memory_space=pltpu.VMEM)
@@ -357,7 +342,7 @@
         out_specs=vmem_spec,
         scratch_shapes=scratch,
         compiler_params=pltpu.CompilerParams(
-            collective_id=0, has_side_effects=True, vmem_limit_bytes=48 * 1024 * 1024
+            collective_id=0, has_side_effects=True, vmem_limit_bytes=60 * 1024 * 1024
         ),
     )(outgoing, w_gate, w_up, w_down)
 

time: 75.6 us -> 71.5 us (0.946)
  Pallas kernels: 67.2 us -> 63.4 us
  local copies, waits for them, and re-layouts: 3.47 us -> 2.49 us
    pallas_call x1, Pallas kernels: 67.2 us -> 63.4 us  [experts(): pl.pallas_call(functools.partial(moe_kernel, ws, nz), out_shape=jax.Shape...]
    unnamed x19 -> x17, local copies, waits for them, and re-layouts: 2.89 us -> 1.01 us
    slice x1, local copies, waits for them, and re-layouts: 0.02 us -> 0.92 us  [per_device(): returned[:, :, end // 8 - w:end // 8].reshape(nz, CAP, 8 * w)]
where the time goes in v3:
time: 71.5 us; the launch traced here: 70.9 us
  Pallas kernels  63.4 us (89%)
  local copies, waits for them, and re-layouts  2.49 us (3%)
  matrix products  2.45 us (3%)
  other arithmetic  2.42 us (3%)
    pallas_call x1, Pallas kernels, experts(): pl.pallas_call(functools.partial(moe_kernel, ws, nz), out_shape=jax.Shape...  63.4 us

profile of v3, /device:TPU:6, one launch (start us, length us, event | category | flops | bytes accessed | tf_op | source)
XLA Modules:
  0.0 70.9 jit_solution(1120767609762285754)
XLA Ops:
  0.0 0.0 copy-start
  0.0 0.0 copy-start.7
  0.0 0.0 copy-start.4
  0.0 0.0 copy-start.6
  0.0 1.0 %copy.36 = bf16[4,48,128]{2,0,1:T(4,128)(2,1)S(1)} copy(bf16[4,48,128]{2,1,0:T(8,128)(2,1)} %param.13) | data formatting | bytes 98304 | tf_op args[0]
  1.0 1.1 %iota_compare_fusion.2 = pred[4,256]{1,0:T(4,128)(4,1)S(1)} fusion(s32[4]{0:T(128)} %param.18), kind=kLoop, calls=%fused_computation.44 | loop fusion | flops 1024 | bytes 1040 | tf_op jit(solution)/shard_map/lt | solution.py:33
  2.0 0.0 copy-done
  2.0 0.7 %fusion.56 = (f32[4,8,6]{2,1,0:T(8,128)S(1)}, f32[4,8,6,256]{3,2,1,0:T(8,128)S(1)}) fusion(bf16[4,256,8,128]{3,2,1,0:T(8,128)(2,1)S(1)} %copy-done, bf16[4,8,6,128]{3,0,2,1:T(4,128)(2,1)S(1)} %bitcast.24, pred[4,256]{1,0:T(4,128)(4,1)S(1)} %iota_compare_fusion.2), kind=kOutput, calls=%fused_computation.62 | convolution fusion | flops 12730176 | bytes 2344704 | tf_op jit(solution)/shard_map/rkgd,rtkd->rkgt/dot_general | solution.py:25
  2.8 0.0 copy-start.1
  2.8 0.0 copy-done.7
  2.8 0.2 fusion.29
  2.9 0.0 copy-start.5
  3.0 0.0 copy-start.2
  3.0 0.2 fusion.21
  3.2 0.0 copy-done.4
  3.2 0.0 copy-done.6
  3.2 0.4 fusion.18
  3.7 0.1 reshape.70
  3.7 0.0 copy-done.1
  3.8 0.2 multiply_reduce_fusion
  3.9 0.0 copy-done.5
  3.9 0.1 fusion.40
  4.1 0.0 copy-done.2
  4.1 0.3 convolution_convert_fusion
  4.4 0.1 copy.40
  4.5 0.1 copy.41
  4.6 0.1 copy.42
  4.8 0.7 pad_maximum_fusion.refs_0_
  5.5 0.0 copy-start.3
  5.5 63.4 %shard_map.127 = bf16[8,16,768]{2,1,0:T(8,128)(2,1)} custom-call(bf16[8,16,768]{2,1,0:T(8,128)(2,1)} %pad_maximum_fusion.refs_0_, bf16[6144,256]{1,0:T(8,128)(2,1)} %bitcast.21, bf16[6144,256]{1,0:T(8,128)(2,1)} %bitcast.22, bf16[256,6144]{1,0:T(8,128)(2,1)} %bitcast.23), custom_call_target="tpu_custom_call" | custom-call | tf_op jit(solution)/shard_map/pallas_call | solution.py:338
  68.8 0.9 %fusion.54 = (bf16[8,16,256]{2,1,0:T(8,128)(2,1)S(1)}, bf16[8,16,256]{2,1,0:T(8,128)(2,1)S(1)}, bf16[8,16,256]{2,1,0:T(8,128)(2,1)S(1)}) fusion(bf16[8,16,768]{2,1,0:T(8,128)(2,1)} %shard_map.127), kind=kLoop, calls=%fused_computation.60 | loop fusion | bytes 393216 | tf_op jit(solution)/shard_map/slice | solution.py:392
  69.9 0.0 copy-done.3
  70.0 0.1 select_reduce_fusion
  70.1 0.9 %fusion.1 = bf16[4,6144]{1,0:T(4,128)(2,1)} fusion(bf16[8,2,2048]{2,0,1:T(8,128)(2,1)S(1)} %copy.45, bf16[8,2,2048]{2,0,1:T(8,128)(2,1)S(1)} %copy.44, bf16[8,2,2048]{2,0,1:T(8,128)(2,1)S(1)} %copy.43, f32[4,6144]{1,0:T(4,128)S(1)} %reshape.70, bf16[4,6144]{1,0:T(4,128)(2,1)S(1)} %copy-done.1, bf16[8,4]{0,1:T(4,128)(2,1)S(1)} %bitcast.28, ...), kind=kOutput, calls=%fused_computation.3 | convolution fusion | flops 1474752 | bytes 393440 | tf_op jit(solution)/shard_map/ecr,ecd->rd/dot_general | solution.py:398
  (20 shorter events, 0.4 us)
Async XLA Ops:
  0.0 2.0 %copy-start = (bf16[4,256,8,128]{3,2,1,0:T(8,128)(2,1)S(1)}, bf16[4,256,8,128]{3,2,1,0:T(8,128)(2,1)}, u32[]{:S(2)}) copy-start(bf16[4,256,8,128]{3,2,1,0:T(8,128)(2,1)} %param.14) | copy-start | bytes 6291460
  0.0 2.8 %copy-start.7 = (bf16[4,8,128]{2,1,0:T(8,128)(2,1)S(1)}, bf16[4,8,128]{2,1,0:T(8,128)(2,1)}, u32[]{:S(2)}) copy-start(bf16[4,8,128]{2,1,0:T(8,128)(2,1)} %param.16) | copy-start | bytes 24580
  0.0 3.2 %copy-start.4 = (bf16[4,8,128]{2,1,0:T(8,128)(2,1)S(1)}, bf16[4,8,128]{2,1,0:T(8,128)(2,1)}, u32[]{:S(2)}) copy-start(bf16[4,8,128]{2,1,0:T(8,128)(2,1)} %param.17) | copy-start | bytes 24580
  0.0 3.2 %copy-start.6 = (bf16[4,256,8,128]{3,2,1,0:T(8,128)(2,1)S(1)}, bf16[4,256,8,128]{3,2,1,0:T(8,128)(2,1)}, u32[]{:S(2)}) copy-start(bf16[4,256,8,128]{3,2,1,0:T(8,128)(2,1)} %param.15) | copy-start | bytes 6291460
  2.8 1.0 %copy-start.1 = (bf16[4,6144]{1,0:T(4,128)(2,1)S(1)}, bf16[4,6144]{1,0:T(4,128)(2,1)}, u32[]{:S(2)}) copy-start(bf16[4,6144]{1,0:T(4,128)(2,1)} %param.19) | copy-start | bytes 147460
  2.9 1.0 %copy-start.5 = (s32[4,2]{0,1:T(2,128)S(1)}, s32[4,2]{0,1:T(2,128)}, u32[]{:S(2)}) copy-start(s32[4,2]{0,1:T(2,128)} %param.21) | copy-start | bytes 100
  3.0 1.1 %copy-start.2 = (f32[6144]{0:T(1024)S(1)}, f32[6144]{0:T(1024)}, u32[]{:S(2)}) copy-start(f32[6144]{0:T(1024)} %param.20) | copy-start | bytes 73732
  5.5 64.5 %copy-start.3 = (f32[4,2]{0,1:T(2,128)S(1)}, f32[4,2]{0,1:T(2,128)}, u32[]{:S(2)}) copy-start(f32[4,2]{0,1:T(2,128)} %param.22) | copy-start | bytes 100

commit v4 on v3

--- a/solution.py
+++ b/solution.py
@@ -9,43 +9,9 @@
 from jax.sharding import PartitionSpec as P
 
 CAP = 2
+CHOICES = 2
 SIDE = 4
 MESH = pl.DeviceIdType.MESH
-
-
-def attend(queries, cache_keys, cache_values, new_keys, new_values, lengths):
-    count = queries.shape[0]
-    kv_heads = cache_keys.shape[2]
-    head_size = cache_keys.shape[3]
-    slots_cached = cache_keys.shape[1]
-    group = queries.shape[1] // kv_heads
-    qvals = queries.reshape(count, kv_heads, group, head_size)
-    score_scale = 1.0 / math.sqrt(head_size)
-    cached = (
-        jnp.einsum("rkgd,rtkd->rkgt", qvals, cache_keys, preferred_element_type=jnp.float32)
-        * score_scale
-    )
-    fresh = (
-        jnp.einsum("rkgd,rkd->rkg", qvals, new_keys, preferred_element_type=jnp.float32)
-        * score_scale
-    )
-    positions = jnp.arange(slots_cached, dtype=jnp.int32)
-    valid = positions[None, :] < lengths[:, None]
-    cached = jnp.where(valid[:, None, None, :], cached, jnp.float32(-1e30))
-    highest = jnp.maximum(jnp.max(cached, axis=-1), fresh)
-    cached_exp = jnp.exp(cached - highest[..., None])
-    fresh_exp = jnp.exp(fresh - highest)
-    total = jnp.sum(cached_exp, axis=-1) + fresh_exp
-    cached_w = (cached_exp / total[..., None]).astype(jnp.bfloat16)
-    fresh_w = (fresh_exp / total).astype(jnp.bfloat16)
-    result = jnp.einsum(
-        "rkgt,rtkd->rkgd", cached_w, cache_values, preferred_element_type=jnp.float32
-    )
-    result = (
-        result
-        + fresh_w.astype(jnp.float32)[..., None] * new_values.astype(jnp.float32)[:, :, None, :]
-    )
-    return result.reshape(count, kv_heads * group * head_size).astype(jnp.bfloat16)
 
 
 def moe_kernel(ws, nz, *refs):
@@ -62,10 +28,12 @@
         del refs[:n]
         return got
 
-    out_in, wg_hbm, wu_hbm, wd_hbm, ret_out = take(5)
+    (lens, routes, logits, queries, new_keys, new_values, residual, gain,
+     keys_hbm, values_hbm, wg_hbm, wu_hbm, wd_hbm, out) = take(14)
+    keys, values, mixed, normed, out_in = take(5)
     wg, wu, wd, acc_g, acc_u, hid = take(6)
     zin, xall, part, t1, t2, t3, zout, zret = [take(nk) for _ in range(8)]
-    (w_sem, zs_s, zs_r, p1_s, p1_r, p2_s, p2_r, fw_s, fw_r,
+    (kv_sem, w_sem, zs_s, zs_r, p1_s, p1_r, p2_s, p2_r, fw_s, fw_r,
      ws_s, ws_r, t1_s, t1_r, tf_s, tf_r, t2_s, t2_r, t3_s, t3_r, zo_s, zo_r) = refs
 
     g = lax.axis_index("grp")
@@ -111,12 +79,119 @@
     friends += [at_z(d) for d in range(1, nz)]
     for dev in friends:
         pl.semaphore_signal(barrier, inc=1, device_id=dev, device_id_type=MESH)
+    cache_copies = [
+        pltpu.make_async_copy(keys_hbm, keys, kv_sem.at[0]),
+        pltpu.make_async_copy(values_hbm, values, kv_sem.at[1]),
+    ]
+    for copy in cache_copies:
+        copy.start()
     weights = ((wg_hbm, wg), (wu_hbm, wu), (wd_hbm, wd))
     own_weights = [
         pltpu.make_async_copy(src, dst.at[g], w_sem.at[n]) for n, (src, dst) in enumerate(weights)
     ]
-    for copy in own_weights:
-        copy.start()
+
+    rows_dev, heads, size = queries.shape
+    kv_heads = new_keys.shape[1]
+    group = heads // kv_heads
+    slots = keys.shape[1]
+
+    def iota(shape, dim):
+        return lax.broadcasted_iota(jnp.int32, shape, dim)
+
+    def dot_t(a, b):
+        return lax.dot_general(a, b, (((1,), (1,)), ((), ())), preferred_element_type=f32)
+
+    def owns(shape):
+        low = (iota(shape, 1) & (kv_heads - 1)) * group
+        head = iota(shape, 0)
+        return (head >= low) & (head < low + group)
+
+    for n in range(heads):
+        mixed[n * rows_dev:(n + 1) * rows_dev, :] = residual[:, n * size:(n + 1) * size].astype(f32)
+
+    for copy in cache_copies:
+        copy.wait()
+
+    for i in range(rows_dev):
+        scale = 1.0 / math.sqrt(size)
+        wide = (heads, slots)
+        valid = owns(wide) & (iota(wide, 1) < lens[i] * kv_heads)
+        cached = jnp.where(valid, dot_t(queries[i], keys[i]) * scale, f32(-1e30))
+        own = owns((heads, kv_heads))
+        fresh = jnp.where(own, dot_t(queries[i], new_keys[i]) * scale, f32(0.0))
+        fresh = jnp.sum(fresh, axis=1, keepdims=True)
+        highest = jnp.maximum(jnp.max(cached, axis=1, keepdims=True), fresh)
+        cached_exp = jnp.exp(cached - highest)
+        fresh_exp = jnp.exp(fresh - highest)
+        share = 1.0 / (jnp.sum(cached_exp, axis=1, keepdims=True) + fresh_exp)
+        cached_w = (cached_exp * share).astype(bf)
+        fresh_w = jnp.where(own, fresh_exp * share, f32(0.0)).astype(bf)
+        attended = jnp.dot(cached_w, values[i], preferred_element_type=f32)
+        attended = attended + jnp.dot(fresh_w, new_values[i], preferred_element_type=f32)
+        request = pl.ds(i, heads, stride=rows_dev)
+        mix = mixed[request, :] + attended.astype(bf).astype(f32)
+        mixed[request, :] = mix
+        square = jnp.sum(jnp.sum(mix * mix, axis=1, keepdims=True), axis=0, keepdims=True)
+        norm = lax.rsqrt(square * (1.0 / (heads * size)) + 1e-05)
+        normed[i] = (mix * norm * gain[...]).astype(bf)
+
+    seat = []
+    for i in range(rows_dev):
+        for c in range(CHOICES):
+            rank = jnp.int32(0)
+            for before in range(i):
+                for other in range(CHOICES):
+                    rank = rank + jnp.where(routes[other, before] == routes[c, i], 1, 0)
+            seat.append(routes[c, i] * CAP + rank)
+
+    per = ws[0] // size
+    pieces = 8 * per
+    shape = (nz * 16, rows_dev * heads)
+    seat_of = iota(shape, 0) >> 3
+    part_of = iota(shape, 0) & 7
+    piece = jnp.zeros(shape, jnp.int32)
+    taken = jnp.zeros(shape, jnp.int32)
+    for i in range(rows_dev):
+        begin = iota(shape, 1) >= i * heads
+        piece = jnp.where(begin, iota(shape, 1) - i * heads, piece)
+        hit = jnp.zeros(shape, jnp.int32)
+        for c in range(CHOICES):
+            hit = jnp.where(seat_of == seat[i * CHOICES + c], 1, hit)
+        taken = jnp.where(begin, hit, taken)
+    piece = jnp.where(taken == 1, piece, -1)
+    flat = normed[...].reshape(rows_dev * heads, size)
+    for k in chunks:
+        for j in range(per):
+            pick = jnp.where(piece == k * pieces + part_of * per + j, f32(1.0), f32(0.0))
+            block = jnp.dot(pick.astype(bf), flat, preferred_element_type=f32).astype(bf)
+            start = (k * per + j) * size
+            out_in[:, :, start:start + size] = block.reshape(nz, 16, size)
+
+    shape = (pieces * rows_dev, nz * 16)
+    seat_of = iota(shape, 1) >> 3
+    part_of = iota(shape, 1) & 7
+    piece = iota(shape, 0) // rows_dev
+    request_of = iota(shape, 0) & (rows_dev - 1)
+    level = [jnp.zeros(shape, f32) for _ in range(CHOICES)]
+    place = [jnp.zeros(shape, jnp.int32) for _ in range(CHOICES)]
+    for i in range(rows_dev):
+        for c in range(CHOICES):
+            level[c] = jnp.where(request_of == i, logits[c, i], level[c])
+            place[c] = jnp.where(request_of == i, seat[i * CHOICES + c], place[c])
+    top = jnp.maximum(level[0], level[1])
+    level = [jnp.exp(v - top) for v in level]
+    mixing = jnp.zeros(shape, f32)
+    for c in range(CHOICES):
+        mixing = mixing + jnp.where(seat_of == place[c], level[c] / (level[0] + level[1]), f32(0.0))
+    weighted = []
+    for j in range(per):
+        term = jnp.where(piece == part_of * per + j, mixing, f32(0.0))
+        split = []
+        for _ in range(3):
+            split.append(term.astype(bf))
+            term = term - split[-1].astype(f32)
+        weighted.append(jnp.concatenate(split, axis=0))
+
     pl.semaphore_wait(barrier, len(friends))
 
     for k in chunks:
@@ -125,6 +200,8 @@
             send(out_in.at[to, :, lanes[k]], zin[k].at[z], zs_s.at[k, d - 1], zs_r.at[k, d - 1], at_z(d))
     for k in chunks:
         zin[k][z] = out_in[z, :, lanes[k]]
+    for copy in own_weights:
+        copy.start()
     for n, (src, dst) in enumerate(weights):
         send(src, dst.at[g], ws_s.at[n], ws_r.at[n], partner)
 
@@ -295,7 +372,19 @@
         for d in z_far_first[::-1]:
             src = (z + nz - d) % nz
             landed(zret[k].at[src], zo_s.at[k, d - 1], zo_r.at[k, d - 1], at_z(nz - d))
-        ret_out[:, :, lanes[k]] = zret[k][...]
+        block = zret[k][...].reshape(units, ws[k])
+        moe = None
+        for j in range(per):
+            piece_sum = jnp.dot(
+                weighted[j], block[:, j * size:(j + 1) * size], preferred_element_type=f32
+            )
+            moe = piece_sum if moe is None else moe + piece_sum
+        count = rows_dev * pieces
+        moe = moe[:count] + moe[count:2 * count] + moe[2 * count:]
+        moe = moe + mixed[k * count:(k + 1) * count, :]
+        for n in range(pieces):
+            start = (k * pieces + n) * size
+            out[:, start:start + size] = moe[n * rows_dev:(n + 1) * rows_dev].astype(bf)
 
     for stage in (a0, a1, a2):
         for k in chunks:
@@ -310,14 +399,19 @@
         copy.wait_send()
 
 
-def experts(outgoing, w_gate, w_up, w_down, ws):
-    nz = outgoing.shape[0]
+def layer(lens, routes, logits, queries, new_keys, new_values, residual, gain, keys, values,
+          w_gate, w_up, w_down, ws, nz):
     nk = len(ws)
     width, slice_size = w_gate.shape
     bf = jnp.bfloat16
     dma = pltpu.SemaphoreType.DMA
     vmem = pltpu.VMEM
     scratch = [
+        vmem(keys.shape, bf),
+        vmem(values.shape, bf),
+        vmem((queries.shape[0] * queries.shape[1], queries.shape[2]), jnp.float32),
+        vmem(queries.shape, bf),
+        vmem((nz, 16, sum(ws)), bf),
         vmem((2, width, slice_size), bf),
         vmem((2, width, slice_size), bf),
         vmem((2, slice_size, width), bf),
@@ -329,7 +423,7 @@
     for lead in ((nz, 16), blocks, blocks, (2, 2, 2, 16), (2, 2, 4, 16),
                  (2, 3, 16), (nz, 16), (nz, 16)):
         scratch += [vmem(lead + ((w if lead[0] == nz else 4 * w),), bf) for w in ws]
-    scratch.append(dma((3,)))
+    scratch += [dma((2,)), dma((3,))]
     for shape in [(nk, nz - 1), (nk, 2, 3), (nk, 2, 2, 4), (nk, 2, 2),
                   (3,), (nk, 2, 2), (nk, 2, 2), (nk, 2, 2), (nk, 2, 3), (nk, nz - 1)]:
         scratch += [dma(shape), dma(shape)]
@@ -337,14 +431,15 @@
     vmem_spec = pl.BlockSpec(memory_space=pltpu.VMEM)
     return pl.pallas_call(
         functools.partial(moe_kernel, ws, nz),
-        out_shape=jax.ShapeDtypeStruct(outgoing.shape, bf),
-        in_specs=[vmem_spec] + [any_spec] * 3,
+        out_shape=jax.ShapeDtypeStruct(residual.shape, bf),
+        in_specs=[pl.BlockSpec(memory_space=pltpu.SMEM)] * 3 + [vmem_spec] * 5 + [any_spec] * 5,
         out_specs=vmem_spec,
         scratch_shapes=scratch,
         compiler_params=pltpu.CompilerParams(
             collective_id=0, has_side_effects=True, vmem_limit_bytes=60 * 1024 * 1024
         ),
-    )(outgoing, w_gate, w_up, w_down)
+    )(lens, routes, logits, queries, new_keys, new_values, residual, gain, keys, values,
+      w_gate, w_up, w_down)
 
 
 def per_device(
@@ -362,41 +457,17 @@
     w_up,
     w_down,
 ):
-    attended = attend(queries, cache_keys, cache_values, new_keys, new_values, lengths)
-    mixed = residual.astype(jnp.float32) + attended.astype(jnp.float32)
-    normed = (
-        mixed * lax.rsqrt(jnp.mean(mixed * mixed, axis=-1, keepdims=True) + 1e-05) * norm_gain
-    ).astype(jnp.bfloat16)
     nz = lax.axis_size("hid")
-    width = normed.shape[1]
+    count, heads, size = queries.shape
+    kv_heads = new_keys.shape[1]
     ws = (256, 256, 256)
-    expert_ids = jnp.arange(nz, dtype=jnp.int32)
-    chosen = routes[:, :, None] == expert_ids[None, None, :]
-    gates = jax.nn.softmax(gate_logits, axis=-1)
-    combine = jnp.sum(jnp.where(chosen, gates[:, :, None], jnp.float32(0.0)), axis=1)
-    selected = jnp.any(chosen, axis=1).astype(jnp.int32)
-    ranking = jnp.cumsum(selected, axis=0) - selected
-    slot_ids = jnp.arange(CAP, dtype=jnp.int32)
-    placement = (selected.T[:, None, :] == 1) & (ranking.T[:, None, :] == slot_ids[None, :, None])
-    outgoing = jnp.einsum(
-        "ecr,rd->ecd", placement.astype(jnp.bfloat16), normed, preferred_element_type=jnp.float32
-    ).astype(jnp.bfloat16)
-    ends = [8 * sum(ws[: k + 1]) for k in range(len(ws))]
-    outgoing = jnp.concatenate(
-        [outgoing[:, :, end - 8 * w:end].reshape(nz, CAP * 8, w) for end, w in zip(ends, ws)],
-        axis=-1,
+    flat_cache = (count, cache_keys.shape[1] * kv_heads, size)
+    return layer(
+        lengths, routes.T, gate_logits.T, queries, new_keys, new_values, residual,
+        norm_gain.reshape(heads, size),
+        cache_keys.reshape(flat_cache), cache_values.reshape(flat_cache),
+        w_gate[0], w_up[0], w_down[0], ws, nz,
     )
-    returned = experts(outgoing, w_gate[0], w_up[0], w_down[0], ws)
-    returned = jnp.concatenate(
-        [
-            returned[:, :, end // 8 - w:end // 8].reshape(nz, CAP, 8 * w)
-            for end, w in zip(ends, ws)
-        ],
-        axis=-1,
-    )
-    mixing = placement.astype(jnp.float32) * combine.T[:, None, :]
-    moe = jnp.einsum("ecr,ecd->rd", mixing, returned.astype(jnp.float32))
-    return (mixed + moe).astype(jnp.bfloat16)
 
 
 def solution(mesh):

time: 71.5 us -> 68.2 us (0.954)
  Pallas kernels: 63.4 us -> 66.6 us
  matrix products: 2.45 us -> 0 us
  other arithmetic: 2.42 us -> 0 us
  local copies, waits for them, and re-layouts: 2.49 us -> 1.44 us
    pallas_call x1, Pallas kernels: 63.4 us -> 66.6 us  [layer(): pl.pallas_call(functools.partial(moe_kernel, ws, nz), out_shape=jax.Shape...]
    dot_general x5 -> x0, matrix products: 2.45 us -> none  [the longest x1 0.86 us: per_device(): moe = jnp.einsum('ecr,ecd->rd', mixing, returned.astype(jnp.float32))]
    slice x5 -> x0, local copies, waits for them, and re-layouts: 1.14 us -> none  [the longest x1 0.92 us: per_device(): returned[:, :, end // 8 - w:end // 8].reshape(nz, CAP, 8 * w)]
    lt x1 -> x0, other arithmetic: 1.05 us -> none  [attend(): valid = positions[None, :] < lengths[:, None]]
    unnamed x17 -> x1, local copies, waits for them, and re-layouts: 1.01 us -> 1.44 us
where the time goes in v4:
time: 68.2 us; the launch traced here: 68 us
  Pallas kernels  66.6 us (98%)
  local copies, waits for them, and re-layouts  1.44 us (2%)
    pallas_call x1, Pallas kernels, layer(): pl.pallas_call(functools.partial(moe_kernel, ws, nz), out_shape=jax.Shape...  66.6 us
    unnamed x1, local copies, waits for them, and re-layouts  1.44 us

profile of v4, /device:TPU:6, one launch (start us, length us, event | category | flops | bytes accessed | tf_op | source)
XLA Modules:
  0.0 68.0 jit_solution(14284000761573022981)
XLA Ops:
  0.0 66.6 %shard_map.127 = bf16[4,6144]{1,0:T(4,128)(2,1)} custom-call(s32[4]{0:T(128)} %refs_0_.1, s32[2,4]{1,0:T(2,128)} %bitcast.14, f32[2,4]{1,0:T(2,128)} %bitcast.15, bf16[4,48,128]{2,1,0:T(8,128)(2,1)} %refs_3_.1, bf16[4,8,128]{2,1,0:T(8,128)(2,1)} %refs_4_.1, bf16[4,8,128]{2,1,0:T(8,128)(2,1)} %refs_5_.1, bf16[4,6144]{1,0:T(4,128)(2,1)} %refs_6_.1, ...), custom_call_target="tpu_custom_call" | custom-call | tf_op jit(solution)/shard_map/pallas_call | solution.py:432
  66.6 1.4 %copy.15 = bf16[4,6144]{1,0:T(4,128)(2,1)} copy(bf16[4,6144]{1,0:T(4,128)(2,1)} %shard_map.127) | data formatting | bytes 98304
